TPU v7x, 128 devices: a whole 4x4x4 slice. The times are simulated.
128 devices in a mesh: ax: 16 (over z, x), az: 8 (over y, core).
Axes of the slice: x: 4, y: 4, z: 4, core: 2. Of those that a mesh axis runs over, the one named last changes fastest.
Arguments:
- history: bfloat16 [8192, 3, 3, 16, 256], P(('ax', 'az')), may hold values from -6 to 6
- inverse_tiles: bfloat16 [8192, 128, 128], P(('ax', 'az')), may hold values from -0.22097087 to 1.2209709
- levels: int32 [8192], P(('ax', 'az')), may hold values from 0 to 2
- destination: int32 [8192], P(('ax', 'az')), may hold values from 0 to 8191, as said below
Outputs:
- new_field: float32 [8192, 3, 16, 256], P(('ax', 'az'))
Inputs may be any that keep to these rules, and one draw needn't show every extreme that they name: `destination`: A permutation of all block places. The 64 blocks of one old owner go to exactly half of all devices as new owners, 1 block to each.
All inputs are finite; a program needn't handle non-finite values.
Results may differ from a plain program's by a relative error of at most 0.009.
Values may be sent and summed in bfloat16 or wider, within the bound.
A program may use at most 128 MiB of HBM per device.

v0:
```python
import jax
import jax.numpy as jnp
from jax import lax
from jax.sharding import PartitionSpec as P

diffusion = 0.04


def with_halo(block, sides, width, periodic):
    for axis, dim in sides:
        count = lax.axis_size(axis)
        forward = [(i, i + 1) for i in range(count - 1)]
        if periodic:
            forward.append((count - 1, 0))
        backward = [(target, source) for source, target in forward]
        low = lax.ppermute(
            lax.slice_in_dim(block, block.shape[dim] - width, None, axis=dim), axis, forward
        )
        high = lax.ppermute(lax.slice_in_dim(block, 0, width, axis=dim), axis, backward)
        block = jnp.concatenate([low, block, high], axis=dim)
    return block


def to_slab(blocks):
    count, comps, edge = (blocks.shape[0], blocks.shape[1], blocks.shape[2])
    shaped = blocks.reshape(count, comps, edge, edge, edge).transpose(1, 2, 3, 0, 4)
    return shaped.reshape(comps, edge, edge, count * edge)


def from_slab(slab_field, count):
    comps, edge = (slab_field.shape[0], slab_field.shape[1])
    shaped = slab_field.reshape(comps, edge, edge, count, edge).transpose(3, 0, 1, 2, 4)
    return shaped.reshape(count, comps, edge, edge * edge)


def combine_history(states):
    past_newest = states[:, 0].astype(jnp.float32)
    combined = (
        18.0 * past_newest
        - 9.0 * states[:, 1].astype(jnp.float32)
        + 2.0 * states[:, 2].astype(jnp.float32)
    )
    return (combined / 11.0).astype(jnp.bfloat16)


def body(history, inverse_tiles, levels, destination):
    block_count = history.shape[0]
    axial_count = lax.axis_size("ax")
    cycle_count = lax.axis_size("az")
    device_count = axial_count * cycle_count
    per_peer = block_count // (device_count // 2)
    slots_total = device_count * per_peer
    owner = destination // block_count
    new_slot = destination % block_count
    serial = jnp.arange(block_count, dtype=jnp.int32)
    same_owner = owner[:, None] == owner[None, :]
    earlier = serial[:, None] > serial[None, :]
    position = owner * per_peer + jnp.sum(same_owner & earlier, axis=1)
    level_scale = jnp.left_shift(jnp.ones_like(levels), 2 * levels).astype(jnp.float32)
    block_meta = jnp.stack(
        [level_scale, (new_slot // 16).astype(jnp.float32), (new_slot % 16).astype(jnp.float32)],
        axis=1,
    ).astype(jnp.bfloat16)

    def pack(values):
        buffer = jnp.zeros((slots_total,) + values.shape[1:], values.dtype).at[position].set(values)
        return buffer.reshape((device_count, per_peer) + values.shape[1:])

    fields_out = pack(history)
    tiles_out = pack(inverse_tiles)
    meta_out = pack(block_meta)
    fields_in, tiles_in, meta_in = (
        lax.all_to_all(fields_out, ("ax", "az"), split_axis=0, concat_axis=0, tiled=True),
        lax.all_to_all(tiles_out, ("ax", "az"), split_axis=0, concat_axis=0, tiled=True),
        lax.all_to_all(meta_out, ("ax", "az"), split_axis=0, concat_axis=0, tiled=True),
    )
    fields_flat = fields_in.reshape((slots_total,) + history.shape[1:])
    tiles_flat = tiles_in.reshape((slots_total,) + inverse_tiles.shape[1:])
    meta_flat = meta_in.reshape(slots_total, 3).astype(jnp.float32)
    filled = meta_flat[:, 0] > 0.0
    target = (meta_flat[:, 1] * 16.0 + meta_flat[:, 2]).astype(jnp.int32)
    target = jnp.where(filled, target, block_count)
    arrived_fields = (
        jnp.zeros((block_count,) + history.shape[1:], jnp.bfloat16)
        .at[target]
        .set(fields_flat, mode="drop")
    )
    arrived_tiles = (
        jnp.zeros(inverse_tiles.shape, jnp.bfloat16).at[target].set(tiles_flat, mode="drop")
    )
    arrived_scale = (
        jnp.zeros((block_count,), jnp.float32).at[target].set(meta_flat[:, 0], mode="drop")
    )
    source_term = combine_history(arrived_fields)
    newest = arrived_fields[:, 0]
    slab_field = to_slab(newest)
    axial_pad = with_halo(slab_field, (("ax", 2),), 1, False)
    cycle_pad = with_halo(slab_field, (("az", 3),), 1, True)
    center = slab_field.astype(jnp.float32)
    radial_pad = jnp.pad(center, ((0, 0), (1, 1), (0, 0), (0, 0)))
    beside_all = radial_pad[:, 2:] + radial_pad[:, :-2]
    beside_all = (
        beside_all
        + axial_pad[:, :, 2:].astype(jnp.float32)
        + axial_pad[:, :, :-2].astype(jnp.float32)
    )
    beside_all = (
        beside_all
        + cycle_pad[:, :, :, 2:].astype(jnp.float32)
        + cycle_pad[:, :, :, :-2].astype(jnp.float32)
    )
    neighbours = from_slab(beside_all, block_count)
    coupling = diffusion * arrived_scale[:, None, None, None]
    newest_value = newest.astype(jnp.float32)
    operated = (1.0 + 6.0 * coupling) * newest_value - coupling * neighbours
    defect = (source_term.astype(jnp.float32) - operated).astype(jnp.bfloat16)
    tile_width = inverse_tiles.shape[1]
    flat_defect = defect.reshape(block_count, -1, tile_width)
    update = jnp.einsum(
        "bpj,bij->bpi", flat_defect, arrived_tiles, preferred_element_type=jnp.float32
    )
    return newest_value + update.reshape(newest_value.shape)


def solution(mesh):
    placed = (
        P(("ax", "az"), None, None, None, None),
        P(("ax", "az"), None, None),
        P(("ax", "az")),
        P(("ax", "az")),
    )
    return jax.shard_map(
        body,
        mesh=mesh,
        in_specs=placed,
        out_specs=P(("ax", "az"), None, None, None),
        check_vma=False,
    )
```

profile of v0, /device:TPU:1, one launch (start us, length us, event | category | flops | bytes accessed | tf_op | source)
XLA Modules:
  0.0 368.6 jit_solution(8474195468899951111)
XLA Ops:
  0.0 0.0 copy-start.1
  0.0 0.8 convert_bitcast_fusion
  0.8 0.7 fusion.17
  1.5 0.1 copy.47
  1.6 0.7 and_select_fusion.3
  2.3 0.2 convert_reduce_fusion
  2.5 0.8 scatter_custom_fusion
  3.2 0.7 copy.48
  3.9 11.5 %all-to-all-start = ((bf16[128,1,3]{2,1,0:T(2,128)(2,1)}), bf16[128,1,3]{2,1,0:T(2,128)(2,1)S(1)}, u32[]{:S(2)}, u32[]{:S(2)}) async-start(bf16[128,1,3]{2,1,0:T(2,128)(2,1)} %copy.48), calls=%async_computation | async-start | bytes 131072 | tf_op jit(solution)/shard_map/all_to_all | solution.py:75
  15.4 3.0 broadcast_in_dim.43
  18.4 0.0 copy-done.1
  18.4 8.6 %scatter_fusion.2 = bf16[128,128,128]{2,1,0:T(8,128)(2,1)} fusion(bf16[128,128,128]{2,1,0:T(8,128)(2,1)} %broadcast_in_dim.43, s32[64]{0:T(128)S(1)} %compare_select_fusion.1, bf16[64,128,128]{2,1,0:T(8,128)(2,1)S(1)} %copy-done.1), kind=kCustom, calls=%fused_computation.4 | custom fusion | bytes 6291712 | tf_op jit(solution)/shard_map/scatter | solution.py:66
  27.0 0.0 all-to-all-done
  27.0 10.3 %all-to-all-start.2 = ((bf16[128,1,128,128]{3,2,1,0:T(8,128)(2,1)}), bf16[128,1,128,128]{3,2,1,0:T(8,128)(2,1)}, u32[]{:S(2)}, u32[]{:S(2)}) async-start(bf16[128,1,128,128]{3,2,1,0:T(8,128)(2,1)} %bitcast.36), calls=%async_computation.2 | async-start | bytes 8388608 | tf_op jit(solution)/shard_map/all_to_all | solution.py:74
  37.3 4.3 %broadcast_in_dim.40 = bf16[128,3,3,16,256]{4,3,2,1,0:T(8,128)(2,1)} broadcast(bf16[]{:T(256)} %constant.65.clone.1), dimensions={} | broadcast | bytes 9437186 | tf_op jit(solution)/shard_map/broadcast_in_dim | solution.py:66
  41.6 12.7 %scatter_fusion = bf16[128,3,3,16,256]{4,3,2,1,0:T(8,128)(2,1)} fusion(bf16[128,3,3,16,256]{4,3,2,1,0:T(8,128)(2,1)} %broadcast_in_dim.40, s32[64]{0:T(128)S(1)} %compare_select_fusion.1, bf16[64,3,3,16,256]{4,3,2,1,0:T(8,128)(2,1)} %param.4), kind=kCustom, calls=%fused_computation.1 | custom fusion | bytes 14156032 | tf_op jit(solution)/shard_map/scatter | solution.py:66
  54.2 35.9 %all-to-all-done.2 = bf16[128,1,128,128]{3,2,1,0:T(8,128)(2,1)} async-done(((bf16[128,1,128,128]{3,2,1,0:T(8,128)(2,1)}), bf16[128,1,128,128]{3,2,1,0:T(8,128)(2,1)}, u32[]{:S(2)}, u32[]{:S(2)}) %all-to-all-start.2) | async-done | bytes 4194336 | tf_op jit(solution)/shard_map/all_to_all | solution.py:74
  90.1 5.5 %all-to-all-start.1 = ((bf16[128,1,3,3,16,256]{5,4,3,2,1,0:T(8,128)(2,1)}), bf16[128,1,3,3,16,256]{5,4,3,2,1,0:T(8,128)(2,1)}, u32[]{:S(2)}, u32[]{:S(2)}) async-start(bf16[128,1,3,3,16,256]{5,4,3,2,1,0:T(8,128)(2,1)} %bitcast.35), calls=%async_computation.1 | async-start | bytes 18874368 | tf_op jit(solution)/shard_map/all_to_all | solution.py:73
  95.6 0.1 convert_element_type.93
  95.7 0.1 slice_reduce_fusion
  95.8 0.2 fusion.9
  96.0 1.0 scatter_custom_fusion.3
  97.0 0.5 broadcast_in_dim.42
  97.5 12.8 %scatter_fusion.3 = bf16[64,128,128]{2,1,0:T(8,128)(2,1)S(1)} fusion(bf16[64,128,128]{2,1,0:T(8,128)(2,1)S(1)} %broadcast_in_dim.42, s32[128]{0:T(128)S(1)} %fusion.9, bf16[128,128,128]{2,1,0:T(8,128)(2,1)} %bitcast.15), kind=kCustom, calls=%fused_computation.5 | custom fusion | bytes 12583424 | tf_op jit(solution)/shard_map/scatter | solution.py:89
  110.2 97.7 %all-to-all-done.1 = bf16[128,1,3,3,16,256]{5,4,3,2,1,0:T(8,128)(2,1)} async-done(((bf16[128,1,3,3,16,256]{5,4,3,2,1,0:T(8,128)(2,1)}), bf16[128,1,3,3,16,256]{5,4,3,2,1,0:T(8,128)(2,1)}, u32[]{:S(2)}, u32[]{:S(2)}) %all-to-all-start.1) | async-done | bytes 9437216 | tf_op jit(solution)/shard_map/all_to_all | solution.py:73
  207.9 2.4 broadcast_in_dim.18
  210.3 23.2 %scatter_fusion.1 = bf16[64,3,3,16,256]{4,3,2,1,0:T(8,128)(2,1)} fusion(bf16[64,3,3,16,256]{4,3,2,1,0:T(8,128)(2,1)} %broadcast_in_dim.18, s32[128]{0:T(128)S(1)} %fusion.9, bf16[128,3,3,16,256]{4,3,2,1,0:T(8,128)(2,1)} %bitcast.7), kind=kCustom, calls=%fused_computation.2 | custom fusion | bytes 28312064 | tf_op jit(solution)/shard_map/scatter | solution.py:86
  233.5 4.1 %slice_convert_fusion = (f32[64,1,3,16,256]{4,3,2,1,0:T(8,128)}, bf16[64,1,3,16,256]{4,3,2,1,0:T(8,128)(2,1)}) fusion(bf16[64,3,3,16,256]{4,3,2,1,0:T(8,128)(2,1)} %scatter_fusion.1), kind=kLoop, calls=%fused_computation.61 | loop fusion | flops 786432 | bytes 6291456 | tf_op jit(solution)/shard_map/convert_element_type | solution.py:114
  237.7 4.6 %copy.50 = bf16[64,1,3,16,256]{0,4,3,2,1:T(8,128)(2,1)} copy(bf16[64,1,3,16,256]{4,3,2,1,0:T(8,128)(2,1)} %get-tuple-element.11) | data formatting | bytes 3145728 | tf_op jit(solution)/shard_map/slice | solution.py:95
  242.2 11.2 %copy.51 = bf16[3,16,16,64,16]{4,3,2,1,0:T(8,128)(2,1)} copy(bf16[3,16,16,64,16]{3,4,2,1,0:T(8,128)(2,1)} %bitcast.38) | data formatting | bytes 3145728 | tf_op jit(solution)/shard_map/transpose | solution.py:26
  253.4 22.8 %reshape.55 = bf16[3,16,16,1024]{3,2,1,0:T(8,128)(2,1)} reshape(bf16[3,16,16,64,16]{4,3,2,1,0:T(8,128)(2,1)} %copy.51) | data formatting | bytes 3145728 | tf_op jit(solution)/shard_map/reshape | solution.py:27
  276.2 1.7 fusion.22
  277.9 1.1 fusion.23
  279.0 0.0 copy-start
  279.0 5.7 %convert_multiply_fusion.1 = (f32[64,1,3,16,256]{4,3,2,1,0:T(8,128)}, f32[64,1,3,16,256]{4,3,2,1,0:T(8,128)}) fusion(bf16[64,3,3,16,256]{4,3,2,1,0:T(8,128)(2,1)} %scatter_fusion.1), kind=kLoop, calls=%fused_computation.15 | loop fusion | flops 3145728 | bytes 9437184 | tf_op jit(solution)/shard_map/mul | solution.py:40
  284.8 1.3 collective-permute-start
  286.0 4.2 %collective-permute-start.1 = (bf16[3,16,1,1024]{3,2,1,0:T(2,128)(2,1)S(1)}, bf16[3,16,1,1024]{3,2,1,0:T(2,128)(2,1)S(1)}, u32[]{:S(2)}, u32[]{:S(2)}) collective-permute-start(bf16[3,16,1,1024]{3,2,1,0:T(2,128)(2,1)S(1)} %get-tuple-element.13), channel_id=1, source_target_pairs={{0,8},{8,16},{16,24},{24,32},{32,40},{40,48},{48,56},{56,64},{64,7... | collective-permute-start | bytes 294920 | tf_op jit(solution)/shard_map/ppermute | solution.py:16
  290.2 0.6 collective-permute-start.2
  290.8 1.2 collective-permute-start.3
  292.0 0.0 copy-done
  292.0 2.2 pad_convert_fusion
  294.2 4.4 %mul.80 = f32[64,96,128]{2,1,0:T(8,128)} reshape(f32[64,1,3,16,256]{4,3,2,1,0:T(8,128)} %get-tuple-element.8) | data formatting | bytes 6291456 | tf_op jit(solution)/shard_map/mul | solution.py:40
  298.6 4.5 %mul.83 = f32[64,96,128]{2,1,0:T(8,128)} reshape(f32[64,1,3,16,256]{4,3,2,1,0:T(8,128)} %get-tuple-element.9) | data formatting | bytes 6291456 | tf_op jit(solution)/shard_map/mul | solution.py:41
  303.1 4.4 %reshape.63 = f32[64,96,128]{2,1,0:T(8,128)} reshape(f32[64,1,3,16,256]{4,3,2,1,0:T(8,128)} %get-tuple-element.10) | data formatting | bytes 6291456 | tf_op jit(solution)/shard_map/convert_element_type | solution.py:114
  307.4 0.0 collective-permute-done.2
  307.5 0.0 collective-permute-done.3
  307.5 0.0 collective-permute-done
  307.5 0.0 collective-permute-done.1
  307.5 8.7 %fusion.3 = f32[3,16,16,1024]{3,2,1,0:T(8,128)} fusion(f32[3,18,16,1024]{3,2,1,0:T(8,128)} %pad_convert_fusion, bf16[3,16,16,1024]{3,2,1,0:T(8,128)(2,1)} %reshape.55, bf16[3,16,16,1]{3,2,1,0:T(8,128)(2,1)} %collective-permute-done.3, bf16[3,16,16,1]{3,2,1,0:T(8,128)(2,1)S(1)} %collective-permute-done.2, ...), kind=kLoop, calls=%fused_computation.10 | loop fusion | flops 16515072 | bytes 11209728 | tf_op jit(solution)/shard_map/add | solution.py:108
  316.2 14.7 %reshape.56 = f32[3,16,16,64,16]{4,3,2,1,0:T(8,128)} reshape(f32[3,16,16,1024]{3,2,1,0:T(8,128)} %fusion.3) | data formatting | bytes 6291456 | tf_op jit(solution)/shard_map/reshape | solution.py:32
  330.8 16.6 %copy.52 = f32[64,3,16,16,16]{0,4,3,2,1:T(8,128)} copy(f32[64,3,16,16,16]{4,0,3,2,1:T(8,128)} %bitcast.34) | data formatting | bytes 6291456 | tf_op jit(solution)/shard_map/transpose | solution.py:32
  347.5 6.5 %copy.53 = f32[64,96,128]{2,1,0:T(8,128)} copy(f32[64,96,128]{0,2,1:T(8,128)} %bitcast.37) | data formatting | bytes 6291456 | tf_op jit(solution)/shard_map/reshape | solution.py:33
  353.9 8.0 %fusion.4 = f32[64,96,128]{2,1,0:T(8,128)} fusion(bf16[64,128,128]{2,1,0:T(8,128)(2,1)S(1)} %scatter_fusion.3, f32[64,96,128]{2,1,0:T(8,128)} %copy.53, f32[64,96,128]{2,1,0:T(8,128)} %reshape.63, f32[64,96,128]{2,1,0:T(8,128)} %mul.83, f32[64,96,128]{2,1,0:T(8,128)} %mul.80, f32[64]{0:T(128)S(1)} %get-tuple-element.17, f32[64]{0:T(128)S(1)} %get-tuple-element.16), kind=kOutput, calls=%fused_computation.17 | convolution fusion | flops 209977344 | bytes 17826304 | tf_op jit(solution)/shard_map/bpj,bij->bpi/dot_general | solution.py:119
  361.9 3.1 reshape.60
  365.0 3.6 bitcast_add_fusion
  (3 shorter events, 0.0 us)
Async XLA Ops:
  0.0 18.4 %copy-start.1 = (bf16[64,128,128]{2,1,0:T(8,128)(2,1)S(1)}, bf16[64,128,128]{2,1,0:T(8,128)(2,1)}, u32[]{:S(2)}) copy-start(bf16[64,128,128]{2,1,0:T(8,128)(2,1)} %param.5) | copy-start | bytes 6291460
  3.9 23.1 %all-to-all-start = ((bf16[128,1,3]{2,1,0:T(2,128)(2,1)}), bf16[128,1,3]{2,1,0:T(2,128)(2,1)S(1)}, u32[]{:S(2)}, u32[]{:S(2)}) async-start(bf16[128,1,3]{2,1,0:T(2,128)(2,1)} %copy.48), calls=%async_computation | async-start | bytes 131072 | tf_op jit(solution)/shard_map/all_to_all | solution.py:75
  27.0 63.1 %all-to-all-start.2 = ((bf16[128,1,128,128]{3,2,1,0:T(8,128)(2,1)}), bf16[128,1,128,128]{3,2,1,0:T(8,128)(2,1)}, u32[]{:S(2)}, u32[]{:S(2)}) async-start(bf16[128,1,128,128]{3,2,1,0:T(8,128)(2,1)} %bitcast.36), calls=%async_computation.2 | async-start | bytes 8388608 | tf_op jit(solution)/shard_map/all_to_all | solution.py:74
  90.1 117.8 %all-to-all-start.1 = ((bf16[128,1,3,3,16,256]{5,4,3,2,1,0:T(8,128)(2,1)}), bf16[128,1,3,3,16,256]{5,4,3,2,1,0:T(8,128)(2,1)}, u32[]{:S(2)}, u32[]{:S(2)}) async-start(bf16[128,1,3,3,16,256]{5,4,3,2,1,0:T(8,128)(2,1)} %bitcast.35), calls=%async_computation.1 | async-start | bytes 18874368 | tf_op jit(solution)/shard_map/all_to_all | solution.py:73
  279.0 13.0 %copy-start = (bf16[3,16,16,1024]{3,2,1,0:T(8,128)(2,1)S(1)}, bf16[3,16,16,1024]{3,2,1,0:T(8,128)(2,1)}, u32[]{:S(2)}) copy-start(bf16[3,16,16,1024]{3,2,1,0:T(8,128)(2,1)} %reshape.55) | copy-start | bytes 4718596
  284.8 22.7 %collective-permute-start = (bf16[3,16,1,1024]{3,2,1,0:T(2,128)(2,1)S(1)}, bf16[3,16,1,1024]{3,2,1,0:T(2,128)(2,1)S(1)}, u32[]{:S(2)}, u32[]{:S(2)}) collective-permute-start(bf16[3,16,1,1024]{3,2,1,0:T(2,128)(2,1)S(1)} %get-tuple-element.12), channel_id=1, source_target_pairs={{8,0},{16,8},{24,16},{32,24},{40,32},{48,40},{56,48},{64,56},{72,6... | collective-permute-start | bytes 294920 | tf_op jit(solution)/shard_map/ppermute | solution.py:19
  286.0 21.4 %collective-permute-start.1 = (bf16[3,16,1,1024]{3,2,1,0:T(2,128)(2,1)S(1)}, bf16[3,16,1,1024]{3,2,1,0:T(2,128)(2,1)S(1)}, u32[]{:S(2)}, u32[]{:S(2)}) collective-permute-start(bf16[3,16,1,1024]{3,2,1,0:T(2,128)(2,1)S(1)} %get-tuple-element.13), channel_id=1, source_target_pairs={{0,8},{8,16},{16,24},{24,32},{32,40},{40,48},{48,56},{56,64},{64,7... | collective-permute-start | bytes 294920 | tf_op jit(solution)/shard_map/ppermute | solution.py:16
  290.2 17.2 %collective-permute-start.2 = (bf16[3,16,16,1]{3,2,1,0:T(8,128)(2,1)S(1)}, bf16[3,16,16,1]{3,2,1,0:T(8,128)(2,1)S(1)}, u32[]{:S(2)}, u32[]{:S(2)}) collective-permute-start(bf16[3,16,16,1]{3,2,1,0:T(8,128)(2,1)S(1)} %get-tuple-element.14), channel_id=1, source_target_pairs={{1,0},{2,1},{3,2},{4,3},{5,4},{6,5},{7,6},{0,7},{9,8},{10,9},{11,1... | collective-permute-start | bytes 4616 | tf_op jit(solution)/shard_map/ppermute | solution.py:19
  290.8 16.6 %collective-permute-start.3 = (bf16[3,16,16,1]{3,2,1,0:T(8,128)(2,1)S(1)}, bf16[3,16,16,1]{3,2,1,0:T(8,128)(2,1)}, u32[]{:S(2)}, u32[]{:S(2)}) collective-permute-start(bf16[3,16,16,1]{3,2,1,0:T(8,128)(2,1)S(1)} %get-tuple-element.15), channel_id=1, source_target_pairs={{0,1},{1,2},{2,3},{3,4},{4,5},{5,6},{6,7},{7,0},{8,9},{9,10},{10,1... | collective-permute-start | bytes 4616 | tf_op jit(solution)/shard_map/ppermute | solution.py:16
where the time goes:
time: 374 us; the launch traced here: 369 us
  local copies, waits for them, and re-layouts  166 us (44%)
  waiting for transfers between devices  134 us (36%)
  starting transfers between devices  34.5 us (9%)
  other arithmetic  26.9 us (7%)
  matrix products  7.96 us (2%)
    all_to_all x1, waiting for transfers between devices, body(): lax.all_to_all(fields_out, ('ax', 'az'), split_axis=0, concat_axis=0, til...  97.7 us
    all_to_all x1, waiting for transfers between devices, body(): lax.all_to_all(tiles_out, ('ax', 'az'), split_axis=0, concat_axis=0, tile...  35.9 us
    scatter x1, local copies, waits for them, and re-layouts, body(): arrived_fields = jnp.zeros((block_count,) + history.shape[1:], jnp.bfloat...  23.2 us
    reshape x1, local copies, waits for them, and re-layouts, to_slab(): return shaped.reshape(comps, edge, edge, count * edge)  22.8 us
    scatter x3, local copies, waits for them, and re-layouts, pack(): jnp.zeros((slots_total,) + values.shape[1:], values.dtype).at[position]  22.1 us
    transpose x1, local copies, waits for them, and re-layouts, from_slab(): slab_field.reshape(comps, edge, edge, count, edge).transpose(3, 0, 1, 2, 4)  16.6 us
    reshape x1, local copies, waits for them, and re-layouts, from_slab(): slab_field.reshape(comps, edge, edge, count, edge).transpose(3, 0, 1, 2, 4)  14.7 us
    scatter x1, local copies, waits for them, and re-layouts, body(): jnp.zeros(inverse_tiles.shape, jnp.bfloat16).at[target]  12.8 us
  transfers between devices with their start and end apart: 7, of which 2 were waited for; matrix products, arithmetic and copies ran while one was open for 16% of the time, Pallas kernels for 0%

commit v1 on v0

v1 whole, which is shorter than its diff:
```python
import functools

import jax
import jax.numpy as jnp
from jax import lax
from jax.experimental import pallas as pl
from jax.experimental.pallas import tpu as pltpu
from jax.sharding import PartitionSpec as P

diffusion = 0.04
MESH = pl.DeviceIdType.MESH
F32 = jnp.float32
BF = jnp.bfloat16

BLOCKS = 64
DEVS = 128
AZ = 8
R1 = 80
STRIDE = 107
UNROLL = 4
NONE = 127


def target_of(ax, az, i):
    o = lax.rem(i * STRIDE, DEVS)
    dc = lax.rem(o, 2)
    dy = lax.rem(lax.div(o, 2), 4)
    dx = lax.rem(lax.div(o, 8), 4)
    dz = lax.div(o, 32)
    z = lax.rem(lax.div(ax, 4) + dz, 4)
    x = lax.rem(lax.rem(ax, 4) + dx, 4)
    y = lax.rem(lax.div(az, 2) + dy, 4)
    c = lax.rem(lax.rem(az, 2) + dc, 2)
    return z * 4 + x, y * 2 + c


def bf16_of(mask):
    return jnp.where(mask, 1.0, 0.0).astype(BF)


def fill_constants(nsel, tsel, weights, ax):
    src = lax.broadcasted_iota(jnp.int32, (256, 256), 0)
    dst = lax.broadcasted_iota(jnp.int32, (256, 256), 1)
    ps, qs = lax.div(src, 16), lax.rem(src, 16)
    pd, qd = lax.div(dst, 16), lax.rem(dst, 16)
    beside = ((ps == pd) & (jnp.abs(qs - qd) == 1)) | ((qs == qd) & (jnp.abs(ps - pd) == 1))
    nsel[:, 0:256] = bf16_of(beside)
    src = lax.broadcasted_iota(jnp.int32, (256, 128), 0)
    kk = lax.rem(lax.broadcasted_iota(jnp.int32, (256, 128), 1), 64)
    plane = jnp.where(kk < 48, 0, 8) + lax.rem(kk, 8)
    pick = jnp.where(
        kk < 16,
        240 + kk,
        jnp.where(kk < 32, kk - 16, plane * 16 + jnp.where(lax.rem(kk, 16) < 8, 15, 0)),
    )
    nsel[:, 256:384] = bf16_of(src == pick)
    row = lax.broadcasted_iota(jnp.int32, (48, 128), 0)
    col = lax.broadcasted_iota(jnp.int32, (48, 128), 1)
    pick = jnp.where(
        row < 16,
        row,
        jnp.where(row < 32, 96 + row, lax.rem(row, 8) * 16 + jnp.where(row < 40, 0, 15)),
    )
    tsel[...] = bf16_of(col == pick)
    kk = lax.rem(lax.broadcasted_iota(jnp.int32, (16, 128), 1), 64)
    weights[0] = bf16_of((kk < 16) & (ax > 0))
    weights[1] = bf16_of((kk >= 16) & (kk < 32) & (ax < 15))
    weights[2] = bf16_of((kk >= 32) & (lax.rem(kk, 16) < 8))
    weights[3] = bf16_of((kk >= 32) & (lax.rem(kk, 16) >= 8))


def kernel(
    hist, tiles, dest, lev, out,
    hbuf, tbuf, msg1, send1, recv1, base, send_a, recv_a, send_b, recv_b, stage, ordf,
    nsel, tsel, weights, vidx, sidx, vinv, sinv, meta_s, meta_r,
    load_sem, ssem, rsem, out_sem,
):
    ax = lax.axis_index("ax")
    az = lax.axis_index("az")
    me = ax * AZ + az
    barrier = pltpu.get_barrier_semaphore()

    def greet(i, carry):
        pl.semaphore_signal(barrier, inc=1, device_id=target_of(ax, az, i), device_id_type=MESH)
        return carry

    lax.fori_loop(1, DEVS, greet, 0)

    load_h = pltpu.make_async_copy(hist, hbuf, load_sem.at[0])
    load_t = pltpu.make_async_copy(tiles, tbuf, load_sem.at[1])
    load_h.start()
    load_t.start()

    lane = lax.broadcasted_iota(jnp.int32, (1, 128), 1)

    def place(b, carry):
        which, slot = carry
        there = dest[b]
        hit = lane == lax.div(there, BLOCKS)
        return jnp.where(hit, b, which), jnp.where(hit, lax.rem(there, BLOCKS), slot)

    which, slot = lax.fori_loop(
        0, BLOCKS, place, (jnp.zeros((1, 128), jnp.int32), jnp.full((1, 128), NONE, jnp.int32))
    )
    vidx[0:1, :] = which
    vidx[1:2, :] = slot
    to_smem = pltpu.make_async_copy(vidx, sidx, load_sem.at[2])
    to_smem.start()
    fill_constants(nsel, tsel, weights, ax)
    to_smem.wait()

    lanes16 = lax.broadcasted_iota(jnp.int32, (16, 128), 1)

    def one_block(b):
        x = hbuf[b, 0:3].reshape(48, 256)
        y = jnp.dot(x, nsel[...], preferred_element_type=F32)
        h0 = x.astype(F32)
        h1 = hbuf[b, 3:6].reshape(48, 256).astype(F32)
        h2 = hbuf[b, 6:9].reshape(48, 256).astype(F32)
        source = ((18.0 * h0 - 9.0 * h1 + 2.0 * h2) * (1.0 / 11.0)).astype(BF).astype(F32)
        level = lev[b]
        scale = jnp.where(level == 0, 1.0, jnp.where(level == 1, 4.0, 16.0)).astype(F32)
        c = diffusion * scale
        radial = lax.rem(lax.broadcasted_iota(jnp.int32, (48, 256), 0), 16)
        beside = y[:, 0:256]
        beside += jnp.where(radial == 0, 0.0, pltpu.roll(h0, 1, 0))
        beside += jnp.where(radial == 15, 0.0, pltpu.roll(h0, 47, 0))
        defect = (source - (1.0 + 6.0 * c) * h0 + c * beside).astype(BF)
        lhs = jnp.concatenate([defect[:, 0:128], defect[:, 128:256], tsel[...]], axis=0)
        u = lax.dot_general(lhs, tbuf[b], (((1,), (1,)), ((), ())), preferred_element_type=F32)
        moved = h0 + jnp.concatenate([u[0:48], u[48:96]], axis=1)
        base[b] = moved.astype(BF).reshape(3, 16, 256)
        msg1[b, 0:48] = (u[96:144] * scale).astype(BF)
        faces = y[:, 256:384]
        msg1[b, 48:64] = jnp.where(lanes16 < 64, faces[0:16], faces[16:32]).astype(BF)
        msg1[b, 64:80] = faces[32:48].astype(BF)

    load_h.wait()
    load_t.wait()

    def some_blocks(n, carry):
        for k in range(UNROLL):
            one_block(n * UNROLL + k)
        return carry

    lax.fori_loop(0, BLOCKS // UNROLL, some_blocks, 0)

    kk16 = lax.rem(lanes16, 64)

    def pack_first(d, meta, first):
        below = jnp.where(d >= AZ, d - AZ, d)
        above = jnp.where(d < DEVS - AZ, d + AZ, d)
        slot_below = jnp.where(d >= AZ, sidx[1, below], NONE)
        slot_above = jnp.where(d < DEVS - AZ, sidx[1, above], NONE)
        meta[d] = jnp.where(lane < 64, sidx[1, d], slot_below * 128 + slot_above)
        own, low, high = sidx[0, d], sidx[0, below], sidx[0, above]
        first[d, 0:48] = msg1[own, 0:48]
        for r in (48, 64):
            first[d, r : r + 16] = jnp.where(
                kk16 < 16,
                msg1[low, r : r + 16].astype(F32),
                jnp.where(
                    kk16 < 32, msg1[high, r : r + 16].astype(F32), msg1[own, r : r + 16].astype(F32)
                ),
            ).astype(BF)

    pack_first(me, meta_r, recv1)
    own = sidx[0, me]
    recv_a[me] = base[own, 0:2]
    recv_b[me] = base[own, 2:3]

    pl.semaphore_wait(barrier, DEVS - 1)

    def push(src, dst, n, where):
        pltpu.make_async_remote_copy(
            src_ref=src, dst_ref=dst, send_sem=ssem.at[n], recv_sem=rsem.at[n],
            device_id=where, device_id_type=MESH,
        ).start()

    def send_first(i, carry):
        tax, taz = target_of(ax, az, i)
        d = tax * AZ + taz
        pack_first(d, meta_s, send1)
        push(meta_s.at[d], meta_r.at[me], 0, (tax, taz))
        push(send1.at[d], recv1.at[me], 1, (tax, taz))
        return carry

    lax.fori_loop(1, DEVS, send_first, 0)

    def send_base(n, send, recv, low, high):
        def one(i, carry):
            tax, taz = target_of(ax, az, i)
            d = tax * AZ + taz
            send[d] = base[sidx[0, d], low:high]
            push(send.at[d], recv.at[me], n, (tax, taz))
            return carry

        lax.fori_loop(1, DEVS, one, 0)

    send_base(2, send_a, recv_a, 0, 2)

    def all_of(ref, sem):
        part = ref.at[pl.ds(0, DEVS - 1)]
        pltpu.make_async_copy(part, part, sem).wait()

    all_of(meta_r, rsem.at[0])

    def unplace(s, carry):
        mine, low, high = carry
        code = meta_r[s]
        mine = jnp.where(code == lane, s, mine)
        low = jnp.where(lax.div(code, 128) == lane - 64, s, low)
        high = jnp.where(lax.rem(code, 128) == lane - 64, s, high)
        return mine, low, high

    zero = jnp.zeros((1, 128), jnp.int32)
    mine, low, high = lax.fori_loop(0, DEVS, unplace, (zero, zero, zero))
    vinv[0:1, :] = mine
    vinv[1:2, :] = low
    vinv[2:3, :] = high
    to_smem = pltpu.make_async_copy(vinv, sinv, load_sem.at[2])
    to_smem.start()
    to_smem.wait()

    all_of(recv1, rsem.at[1])

    def order(j, carry):
        ordf[j + 1] = recv1[sinv[0, j], 48:80]
        return carry

    lax.fori_loop(0, BLOCKS, order, 0)
    edge_up = pltpu.make_async_remote_copy(
        src_ref=ordf.at[BLOCKS], dst_ref=ordf.at[0], send_sem=ssem.at[4], recv_sem=rsem.at[4],
        device_id=(ax, lax.rem(az + 1, AZ)), device_id_type=MESH,
    )
    edge_down = pltpu.make_async_remote_copy(
        src_ref=ordf.at[1], dst_ref=ordf.at[BLOCKS + 1], send_sem=ssem.at[5], recv_sem=rsem.at[5],
        device_id=(ax, lax.rem(az + AZ - 1, AZ)), device_id_type=MESH,
    )
    edge_up.start()
    edge_down.start()

    send_base(3, send_b, recv_b, 2, 3)
    edge_up.wait_recv()
    edge_down.wait_recv()

    def correct(j):
        s, s_low, s_high = sinv[0, j], sinv[1, j + 64], sinv[2, j + 64]
        parts = []
        for r in (0, 16):
            parts.append(
                recv1[s_low, 48 + r : 64 + r] * weights[0]
                + recv1[s_high, 48 + r : 64 + r] * weights[1]
                + ordf[j, r : r + 16] * weights[2]
                + ordf[j + 2, r : r + 16] * weights[3]
            )
        lhs = jnp.concatenate([parts[0][:, 0:64], parts[0][:, 64:128], parts[1][:, 0:64]], axis=0)
        none = jnp.zeros((16, 128), BF)
        t_low, t_high, t_side = recv1[s, 0:16], recv1[s, 16:32], recv1[s, 32:48]
        rhs = jnp.concatenate(
            [
                jnp.concatenate([t_low, none, t_side, none], axis=0),
                jnp.concatenate([none, t_high, none, t_side], axis=0),
            ],
            axis=1,
        )
        update = jnp.dot(lhs, rhs, preferred_element_type=F32) * diffusion
        stage[j] = update.reshape(3, 16, 256)

    def some_corrections(n, carry):
        for k in range(UNROLL):
            correct(n * UNROLL + k)
        return carry

    lax.fori_loop(0, BLOCKS // UNROLL, some_corrections, 0)

    all_of(recv_a, rsem.at[2])

    def add_a(n, carry):
        for k in range(UNROLL):
            j = n * UNROLL + k
            stage[j, 0:2] += recv_a[sinv[0, j]].astype(F32)
        return carry

    lax.fori_loop(0, BLOCKS // UNROLL, add_a, 0)
    all_of(recv_b, rsem.at[3])

    def add_b(n, carry):
        for k in range(UNROLL):
            j = n * UNROLL + k
            stage[j, 2:3] += recv_b[sinv[0, j]].astype(F32)
        return carry

    copies = []
    for g in range(4):
        lax.fori_loop(g * 16 // UNROLL, (g + 1) * 16 // UNROLL, add_b, 0)
        part = pl.ds(g * 16, 16)
        copies.append(pltpu.make_async_copy(stage.at[part], out.at[part], out_sem.at[g]))
        copies[-1].start()

    all_of(meta_s, ssem.at[0])
    all_of(send1, ssem.at[1])
    all_of(send_a, ssem.at[2])
    all_of(send_b, ssem.at[3])
    edge_up.wait_send()
    edge_down.wait_send()
    for copy in copies:
        copy.wait()


def body(history, inverse_tiles, levels, destination):
    anywhere = pl.BlockSpec(memory_space=pl.ANY)
    scalars = pl.BlockSpec(memory_space=pltpu.SMEM)
    return pl.pallas_call(
        kernel,
        out_shape=jax.ShapeDtypeStruct((BLOCKS, 3, 16, 256), F32),
        in_specs=[anywhere, anywhere, scalars, scalars],
        out_specs=anywhere,
        scratch_shapes=[
            pltpu.VMEM((BLOCKS, 9, 16, 256), BF),
            pltpu.VMEM((BLOCKS, 128, 128), BF),
            pltpu.VMEM((BLOCKS, R1, 128), BF),
            pltpu.VMEM((DEVS, R1, 128), BF),
            pltpu.VMEM((DEVS, R1, 128), BF),
            pltpu.VMEM((BLOCKS, 3, 16, 256), BF),
            pltpu.VMEM((DEVS, 2, 16, 256), BF),
            pltpu.VMEM((DEVS, 2, 16, 256), BF),
            pltpu.VMEM((DEVS, 1, 16, 256), BF),
            pltpu.VMEM((DEVS, 1, 16, 256), BF),
            pltpu.VMEM((BLOCKS, 3, 16, 256), F32),
            pltpu.VMEM((BLOCKS + 2, 32, 128), BF),
            pltpu.VMEM((256, 384), BF),
            pltpu.VMEM((48, 128), BF),
            pltpu.VMEM((4, 16, 128), BF),
            pltpu.VMEM((8, 128), jnp.int32),
            pltpu.SMEM((8, 128), jnp.int32),
            pltpu.VMEM((8, 128), jnp.int32),
            pltpu.SMEM((8, 128), jnp.int32),
            pltpu.VMEM((DEVS, 1, 128), jnp.int32),
            pltpu.VMEM((DEVS, 1, 128), jnp.int32),
            pltpu.SemaphoreType.DMA((3,)),
            pltpu.SemaphoreType.DMA((6,)),
            pltpu.SemaphoreType.DMA((6,)),
            pltpu.SemaphoreType.DMA((4,)),
        ],
        compiler_params=pltpu.CompilerParams(
            collective_id=0, has_side_effects=True, vmem_limit_bytes=48 * 2**20
        ),
    )(history.reshape(BLOCKS, 9, 16, 256), inverse_tiles, destination, levels)


def solution(mesh):
    placed = (
        P(("ax", "az"), None, None, None, None),
        P(("ax", "az"), None, None),
        P(("ax", "az")),
        P(("ax", "az")),
    )
    return jax.shard_map(
        body,
        mesh=mesh,
        in_specs=placed,
        out_specs=P(("ax", "az"), None, None, None),
        check_vma=False,
    )
```

time: 374 us -> 94.2 us (0.25); the launches traced: 369 us -> 93.7 us
  local copies, waits for them, and re-layouts: 166 us -> 4.57 us
  waiting for transfers between devices: 134 us -> 0 us
  Pallas kernels: 0 us -> 89.1 us
  starting transfers between devices: 34.5 us -> 0 us
  other arithmetic: 26.9 us -> 0 us
  matrix products: 7.96 us -> 0 us
    all_to_all x3 -> x0, waiting for transfers between devices: 134 us -> none  [the longest x1 97.7 us: body(): lax.all_to_all(fields_out, ('ax', 'az'), split_axis=0, concat_axis=0, til...]
    pallas_call x0 -> x1, Pallas kernels: none -> 89.1 us  [body(): pl.pallas_call(kernel, out_shape=jax.ShapeDtypeStruct((BLOCKS, 3, 16, 256...]
    scatter x6 -> x0, local copies, waits for them, and re-layouts: 59 us -> none  [the longest x1 23.2 us: body(): arrived_fields = jnp.zeros((block_count,) + history.shape[1:], jnp.bfloat...]
    reshape x5 -> x0, local copies, waits for them, and re-layouts: 47.7 us -> none  [the longest x1 22.8 us: to_slab(): return shaped.reshape(comps, edge, edge, count * edge)]
    transpose x2 -> x0, local copies, waits for them, and re-layouts: 27.8 us -> none  [the longest x1 16.6 us: from_slab(): slab_field.reshape(comps, edge, edge, count, edge).transpose(3, 0, 1, 2, 4)]
    all_to_all x3 -> x0, starting transfers between devices: 27.2 us -> none  [the longest x1 11.5 us: body(): lax.all_to_all(meta_out, ('ax', 'az'), split_axis=0, concat_axis=0, tiled...]
    add x3 -> x0, other arithmetic: 12.3 us -> none  [the longest x1 8.68 us: body(): beside_all + cycle_pad[:, :, :, 2:].astype(jnp.float32)]
    broadcast_in_dim x4 -> x0, local copies, waits for them, and re-layouts: 10.1 us -> none  [the longest x2 7.24 us: pack(): jnp.zeros((slots_total,) + values.shape[1:], values.dtype).at[position]]
  transfers between devices with their start and end apart: 7 -> 0, of which waited for: 2 -> 0; matrix products, arithmetic and copies ran while one was open for 16% -> 0% of each run, Pallas kernels for 0% -> 0%
where the time goes in v1:
time: 94.2 us; the launch traced here: 93.7 us
  Pallas kernels  89.1 us (95%)
  local copies, waits for them, and re-layouts  4.57 us (5%)
    pallas_call x1, Pallas kernels, body(): pl.pallas_call(kernel, out_shape=jax.ShapeDtypeStruct((BLOCKS, 3, 16, 256...  89.1 us
    unnamed x7, local copies, waits for them, and re-layouts  4.57 us

profile of v1, /device:TPU:1, one launch (start us, length us, event | category | flops | bytes accessed | tf_op | source)
XLA Modules:
  0.0 93.7 jit_solution(6587434330566535996)
XLA Ops:
  0.0 0.0 copy-start
  0.0 1.6 %copy-done = bf16[64,128,128]{2,1,0:T(8,128)(2,1)S(1)} copy-done((bf16[64,128,128]{2,1,0:T(8,128)(2,1)S(1)}, bf16[64,128,128]{2,1,0:T(8,128)(2,1)}, u32[]{:S(2)}) %copy-start) | copy-done | bytes 2097176
  1.6 0.0 copy-start.1
  1.6 0.7 copy-done.1
  2.2 0.0 copy-start.2
  2.2 0.7 copy-done.2
  2.9 89.1 %shard_map.46 = f32[64,3,16,256]{3,2,1,0:T(8,128)S(1)} custom-call(bf16[64,9,16,256]{3,2,1,0:T(8,128)(2,1)} %bitcast.1, bf16[64,128,128]{2,1,0:T(8,128)(2,1)S(1)} %copy-done, s32[64]{0:T(128)S(1)} %copy-done.1, s32[64]{0:T(128)S(1)} %copy-done.2), custom_call_target="tpu_custom_call" | custom-call | tf_op jit(solution)/shard_map/pallas_call | solution.py:314
  92.0 1.7 %copy.6 = f32[64,3,16,256]{3,2,1,0:T(8,128)} copy(f32[64,3,16,256]{3,2,1,0:T(8,128)S(1)} %shard_map.46) | data formatting | bytes 6291456
Async XLA Ops:
  0.0 1.6 %copy-start = (bf16[64,128,128]{2,1,0:T(8,128)(2,1)S(1)}, bf16[64,128,128]{2,1,0:T(8,128)(2,1)}, u32[]{:S(2)}) copy-start(bf16[64,128,128]{2,1,0:T(8,128)(2,1)} %tiles.1) | copy-start | bytes 6291460
  1.6 0.7 copy-start.1
  2.2 0.7 copy-start.2

commit v2 on v1

v2 whole, which is shorter than its diff:
```python
import functools

import jax
import jax.numpy as jnp
from jax import lax
from jax.experimental import pallas as pl
from jax.experimental.pallas import tpu as pltpu
from jax.sharding import PartitionSpec as P

diffusion = 0.04
MESH = pl.DeviceIdType.MESH
F32 = jnp.float32
BF = jnp.bfloat16

BLOCKS = 64
DEVS = 128
AZ = 8
R1 = 80
STRIDE = 107
UNROLL = 4
NONE = 127


def target_of(ax, az, i):
    o = lax.rem(i * STRIDE, DEVS)
    dc = lax.rem(o, 2)
    dy = lax.rem(lax.div(o, 2), 4)
    dx = lax.rem(lax.div(o, 8), 4)
    dz = lax.div(o, 32)
    z = lax.rem(lax.div(ax, 4) + dz, 4)
    x = lax.rem(lax.rem(ax, 4) + dx, 4)
    y = lax.rem(lax.div(az, 2) + dy, 4)
    c = lax.rem(lax.rem(az, 2) + dc, 2)
    return z * 4 + x, y * 2 + c


def bf16_of(mask):
    return jnp.where(mask, 1.0, 0.0).astype(BF)


def fill_constants(nsel, fsel, tsel, weights, ax):
    src = lax.broadcasted_iota(jnp.int32, (256, 256), 0)
    dst = lax.broadcasted_iota(jnp.int32, (256, 256), 1)
    ps, qs = lax.div(src, 16), lax.rem(src, 16)
    pd, qd = lax.div(dst, 16), lax.rem(dst, 16)
    beside = ((ps == pd) & (jnp.abs(qs - qd) == 1)) | ((qs == qd) & (jnp.abs(ps - pd) == 1))
    nsel[...] = bf16_of(beside)
    src = lax.broadcasted_iota(jnp.int32, (256, 128), 0)
    kk = lax.rem(lax.broadcasted_iota(jnp.int32, (256, 128), 1), 64)
    plane = jnp.where(kk < 48, 0, 8) + lax.rem(kk, 8)
    pick = jnp.where(
        kk < 16,
        240 + kk,
        jnp.where(kk < 32, kk - 16, plane * 16 + jnp.where(lax.rem(kk, 16) < 8, 15, 0)),
    )
    low, high = kk < 16, (kk >= 16) & (kk < 32)
    fsel[0] = bf16_of((src == pick) & low)
    fsel[1] = bf16_of((src == pick) & high)
    fsel[2] = bf16_of((src == pick) & (kk >= 32))
    row = lax.broadcasted_iota(jnp.int32, (48, 128), 0)
    col = lax.broadcasted_iota(jnp.int32, (48, 128), 1)
    pick = jnp.where(
        row < 16,
        row,
        jnp.where(row < 32, 96 + row, lax.rem(row, 8) * 16 + jnp.where(row < 40, 0, 15)),
    )
    tsel[...] = bf16_of(col == pick)
    kk = lax.rem(lax.broadcasted_iota(jnp.int32, (16, 128), 1), 64)
    weights[0] = bf16_of((kk < 16) & (ax > 0))
    weights[1] = bf16_of((kk >= 16) & (kk < 32) & (ax < 15))
    weights[2] = bf16_of((kk >= 32) & (lax.rem(kk, 16) < 8))
    weights[3] = bf16_of((kk >= 32) & (lax.rem(kk, 16) >= 8))


def kernel(
    hist, tiles, dest_any, lev_any, out,
    newest, older, tbuf, send1, recv1, base, send_a, recv_a, send_b, recv_b, stage, final, ordf,
    nsel, fsel, tsel, weights, dest, lev, vidx, sidx, vinv, sinv,
    load_sem, ssem, rsem, out_sem,
):
    ax = lax.axis_index("ax")
    az = lax.axis_index("az")
    me = ax * AZ + az
    barrier = pltpu.get_barrier_semaphore()

    load_d = pltpu.make_async_copy(dest_any, dest, load_sem.at[3])
    load_l = pltpu.make_async_copy(lev_any, lev, load_sem.at[4])
    load_h0 = pltpu.make_async_copy(hist.at[:, pl.ds(0, 3)], newest, load_sem.at[0])
    load_h = pltpu.make_async_copy(hist.at[:, pl.ds(3, 6)], older, load_sem.at[5])
    load_t = pltpu.make_async_copy(tiles, tbuf, load_sem.at[1])
    loads = (load_d, load_l, load_h0, load_t, load_h)
    for load in loads:
        load.start()

    def greet(i, carry):
        t = lax.rem(me + i, DEVS)
        there = (lax.div(t, AZ), lax.rem(t, AZ))
        pl.semaphore_signal(barrier, inc=1, device_id=there, device_id_type=MESH)
        return carry

    lax.fori_loop(1, DEVS, greet, 0)

    lane = lax.broadcasted_iota(jnp.int32, (1, 128), 1)

    def place(b, carry):
        which, slot = carry
        there = dest[b]
        hit = lane == lax.div(there, BLOCKS)
        return jnp.where(hit, b, which), jnp.where(hit, lax.rem(there, BLOCKS), slot)

    load_d.wait()
    load_l.wait()
    which, slot = lax.fori_loop(
        0, BLOCKS, place, (jnp.zeros((1, 128), jnp.int32), jnp.full((1, 128), NONE, jnp.int32))
    )
    vidx[0:1, :] = which
    vidx[1:2, :] = slot
    to_smem = pltpu.make_async_copy(vidx, sidx, load_sem.at[2])
    to_smem.start()
    fill_constants(nsel, fsel, tsel, weights, ax)
    to_smem.wait()

    lanes16 = lax.broadcasted_iota(jnp.int32, (16, 128), 1)

    def scale_of(b):
        level = lev[b]
        return jnp.where(level == 0, 1.0, jnp.where(level == 1, 4.0, 16.0)).astype(F32)

    def base_part(b):
        x = newest[b].reshape(48, 256)
        h0 = x.astype(F32)
        h1 = older[b, 0:3].reshape(48, 256).astype(F32)
        h2 = older[b, 3:6].reshape(48, 256).astype(F32)
        source = ((18.0 * h0 - 9.0 * h1 + 2.0 * h2) * (1.0 / 11.0)).astype(BF).astype(F32)
        c = diffusion * scale_of(b)
        radial = lax.rem(lax.broadcasted_iota(jnp.int32, (48, 256), 0), 16)
        beside = jnp.dot(x, nsel[...], preferred_element_type=F32)
        beside += jnp.where(radial == 0, 0.0, pltpu.roll(h0, 1, 0))
        beside += jnp.where(radial == 15, 0.0, pltpu.roll(h0, 47, 0))
        defect = (source - (1.0 + 6.0 * c) * h0 + c * beside).astype(BF)
        lhs = jnp.concatenate([defect[:, 0:128], defect[:, 128:256]], axis=0)
        u = lax.dot_general(lhs, tbuf[b], (((1,), (1,)), ((), ())), preferred_element_type=F32)
        moved = h0 + jnp.concatenate([u[0:48], u[48:96]], axis=1)
        base[b] = moved.astype(BF).reshape(3, 16, 256)

    def for_each(count, step):
        def some(n, carry):
            for k in range(UNROLL):
                step(n * UNROLL + k)
            return carry

        lax.fori_loop(0, count // UNROLL, some, 0)

    row16 = lax.broadcasted_iota(jnp.int32, (16, 128), 0)

    def pack_first(d):
        below = jnp.maximum(d - AZ, 0)
        above = jnp.minimum(d + AZ, DEVS - 1)
        slot_below = jnp.where(d >= AZ, sidx[1, below], NONE)
        slot_above = jnp.where(d < DEVS - AZ, sidx[1, above], NONE)
        slots = jnp.where(row16 == 0, sidx[1, d], jnp.where(row16 == 1, slot_below, slot_above))
        own, low, high = sidx[0, d], sidx[0, below], sidx[0, above]
        u = lax.dot_general(tsel[...], tbuf[own], (((1,), (1,)), ((), ())), preferred_element_type=F32)
        send1[d, 0:48] = (u * scale_of(own)).astype(BF)
        faces = sum(
            jnp.dot(newest[b].reshape(48, 256), fsel[n], preferred_element_type=F32)
            for n, b in enumerate((low, high, own))
        )
        send1[d, 48:64] = jnp.where(lanes16 < 64, faces[0:16], faces[16:32]).astype(BF)
        send1[d, 64:80] = jnp.where(lanes16 < 64, faces[32:48], slots.astype(F32)).astype(BF)

    def push(src, dst, n, where):
        pltpu.make_async_remote_copy(
            src_ref=src, dst_ref=dst, send_sem=ssem.at[n], recv_sem=rsem.at[n],
            device_id=where, device_id_type=MESH,
        ).start()

    load_h0.wait()
    load_t.wait()
    pl.semaphore_wait(barrier, DEVS - 1)

    def send_first(n, carry):
        targets = [target_of(ax, az, n * UNROLL + k) for k in range(UNROLL)]
        for tax, taz in targets:
            pack_first(tax * AZ + taz)
        for k, (tax, taz) in enumerate(targets):
            if k > 0:
                push(send1.at[tax * AZ + taz], recv1.at[me], 1, (tax, taz))
            else:

                @pl.when(n > 0)
                def _():
                    push(send1.at[tax * AZ + taz], recv1.at[me], 1, (tax, taz))

        return carry

    lax.fori_loop(0, DEVS // UNROLL, send_first, 0)
    recv1[me] = send1[me]

    load_h.wait()
    for_each(BLOCKS, base_part)
    own = sidx[0, me]
    recv_a[me] = base[own, 0:2]
    recv_b[me] = base[own, 2:3]

    def send_base(n, send, recv, low, high):
        def one(i, carry):
            tax, taz = target_of(ax, az, i)
            d = tax * AZ + taz
            send[d] = base[sidx[0, d], low:high]
            push(send.at[d], recv.at[me], n, (tax, taz))
            return carry

        lax.fori_loop(1, DEVS, one, 0)

    send_base(2, send_a, recv_a, 0, 2)

    def all_of(ref, sem):
        part = ref.at[pl.ds(0, DEVS - 1)]
        pltpu.make_async_copy(part, part, sem).wait()

    all_of(recv1, rsem.at[1])

    slot_of_lane = (lanes16 - 64).astype(F32)

    def unplace(n, found):
        for k in range(UNROLL):
            s = n * UNROLL + k
            found = jnp.where(recv1[s, 64:80].astype(F32) == slot_of_lane, s, found)
        return found

    vinv[...] = lax.fori_loop(0, DEVS // UNROLL, unplace, jnp.zeros((16, 128), jnp.int32))
    to_smem = pltpu.make_async_copy(vinv, sinv, load_sem.at[2])
    to_smem.start()
    to_smem.wait()

    def order(j):
        ordf[j + 1] = recv1[sinv[0, j + 64], 48:80]

    for_each(BLOCKS, order)
    edge_up = pltpu.make_async_remote_copy(
        src_ref=ordf.at[BLOCKS], dst_ref=ordf.at[0], send_sem=ssem.at[4], recv_sem=rsem.at[4],
        device_id=(ax, lax.rem(az + 1, AZ)), device_id_type=MESH,
    )
    edge_down = pltpu.make_async_remote_copy(
        src_ref=ordf.at[1], dst_ref=ordf.at[BLOCKS + 1], send_sem=ssem.at[5], recv_sem=rsem.at[5],
        device_id=(ax, lax.rem(az + AZ - 1, AZ)), device_id_type=MESH,
    )
    edge_up.start()
    edge_down.start()

    send_base(3, send_b, recv_b, 2, 3)
    edge_up.wait_recv()
    edge_down.wait_recv()

    def correct(j):
        s, s_low, s_high = sinv[0, j + 64], sinv[1, j + 64], sinv[2, j + 64]
        parts = []
        for r in (0, 16):
            parts.append(
                recv1[s_low, 48 + r : 64 + r] * weights[0]
                + recv1[s_high, 48 + r : 64 + r] * weights[1]
                + ordf[j, r : r + 16] * weights[2]
                + ordf[j + 2, r : r + 16] * weights[3]
            )
        lhs = jnp.concatenate([parts[0][:, 0:64], parts[0][:, 64:128], parts[1][:, 0:64]], axis=0)
        none = jnp.zeros((16, 128), BF)
        t_low, t_high, t_side = recv1[s, 0:16], recv1[s, 16:32], recv1[s, 32:48]
        rhs = jnp.concatenate(
            [
                jnp.concatenate([t_low, none, t_side, none], axis=0),
                jnp.concatenate([none, t_high, none, t_side], axis=0),
            ],
            axis=1,
        )
        update = jnp.dot(lhs, rhs, preferred_element_type=F32) * diffusion
        stage[j] = update.reshape(3, 16, 256)

    for_each(BLOCKS, correct)

    all_of(recv_a, rsem.at[2])

    def add_a(j):
        final[j, 0:2] = (stage[j, 0:2] + recv_a[sinv[0, j + 64]].astype(F32)).astype(BF)

    for_each(BLOCKS, add_a)
    all_of(recv_b, rsem.at[3])

    def add_b(n, carry):
        for k in range(UNROLL):
            j = n * UNROLL + k
            final[j, 2:3] = (stage[j, 2:3] + recv_b[sinv[0, j + 64]].astype(F32)).astype(BF)
        return carry

    copies = []
    for g in range(4):
        lax.fori_loop(g * 16 // UNROLL, (g + 1) * 16 // UNROLL, add_b, 0)
        part = pl.ds(g * 16, 16)
        copies.append(pltpu.make_async_copy(final.at[part], out.at[part], out_sem.at[g]))
        copies[-1].start()

    all_of(send1, ssem.at[1])
    all_of(send_a, ssem.at[2])
    all_of(send_b, ssem.at[3])
    edge_up.wait_send()
    edge_down.wait_send()
    for copy in copies:
        copy.wait()


def body(history, inverse_tiles, levels, destination):
    anywhere = pl.BlockSpec(memory_space=pl.ANY)
    moved = pl.pallas_call(
        kernel,
        out_shape=jax.ShapeDtypeStruct((BLOCKS, 3, 16, 256), BF),
        in_specs=[pl.BlockSpec(memory_space=pltpu.HBM)] * 4,
        out_specs=anywhere,
        scratch_shapes=[
            pltpu.VMEM((BLOCKS, 3, 16, 256), BF),
            pltpu.VMEM((BLOCKS, 6, 16, 256), BF),
            pltpu.VMEM((BLOCKS, 128, 128), BF),
            pltpu.VMEM((DEVS, R1, 128), BF),
            pltpu.VMEM((DEVS, R1, 128), BF),
            pltpu.VMEM((BLOCKS, 3, 16, 256), BF),
            pltpu.VMEM((DEVS, 2, 16, 256), BF),
            pltpu.VMEM((DEVS, 2, 16, 256), BF),
            pltpu.VMEM((DEVS, 1, 16, 256), BF),
            pltpu.VMEM((DEVS, 1, 16, 256), BF),
            pltpu.VMEM((BLOCKS, 3, 16, 256), F32),
            pltpu.VMEM((BLOCKS, 3, 16, 256), BF),
            pltpu.VMEM((BLOCKS + 2, 32, 128), BF),
            pltpu.VMEM((256, 256), BF),
            pltpu.VMEM((3, 256, 128), BF),
            pltpu.VMEM((48, 128), BF),
            pltpu.VMEM((4, 16, 128), BF),
            pltpu.SMEM((BLOCKS,), jnp.int32),
            pltpu.SMEM((BLOCKS,), jnp.int32),
            pltpu.VMEM((8, 128), jnp.int32),
            pltpu.SMEM((8, 128), jnp.int32),
            pltpu.VMEM((16, 128), jnp.int32),
            pltpu.SMEM((16, 128), jnp.int32),
            pltpu.SemaphoreType.DMA((6,)),
            pltpu.SemaphoreType.DMA((6,)),
            pltpu.SemaphoreType.DMA((6,)),
            pltpu.SemaphoreType.DMA((4,)),
        ],
        compiler_params=pltpu.CompilerParams(
            collective_id=0, has_side_effects=True, vmem_limit_bytes=60 * 2**20
        ),
    )(history.reshape(BLOCKS, 9, 16, 256), inverse_tiles, destination, levels)
    return moved.astype(F32)


def solution(mesh):
    placed = (
        P(("ax", "az"), None, None, None, None),
        P(("ax", "az"), None, None),
        P(("ax", "az")),
        P(("ax", "az")),
    )
    return jax.shard_map(
        body,
        mesh=mesh,
        in_specs=placed,
        out_specs=P(("ax", "az"), None, None, None),
        check_vma=False,
    )
```

time: 94.2 us -> 81.3 us (0.86)
  Pallas kernels: 89.1 us -> 77.7 us
  local copies, waits for them, and re-layouts: 4.57 us -> 0 us
  other arithmetic: 0 us -> 3.52 us
    pallas_call x1, Pallas kernels: 89.1 us -> 77.7 us  [body(): pl.pallas_call(kernel, out_shape=jax.ShapeDtypeStruct((BLOCKS, 3, 16, 256...]
    unnamed x7 -> x0, local copies, waits for them, and re-layouts: 4.57 us -> none
    convert_element_type x0 -> x1, other arithmetic: none -> 3.52 us  [body(): return moved.astype(F32)]
where the time goes in v2:
time: 81.3 us; the launch traced here: 81.2 us
  Pallas kernels  77.7 us (96%)
  other arithmetic  3.52 us (4%)
    pallas_call x1, Pallas kernels, body(): pl.pallas_call(kernel, out_shape=jax.ShapeDtypeStruct((BLOCKS, 3, 16, 256...  77.7 us
    convert_element_type x1, other arithmetic, body(): return moved.astype(F32)  3.52 us

profile of v2, /device:TPU:1, one launch (start us, length us, event | category | flops | bytes accessed | tf_op | source)
XLA Modules:
  0.0 81.2 jit_solution(13549477581060458433)
XLA Ops:
  0.0 77.7 %shard_map.46 = bf16[64,3,16,256]{3,2,1,0:T(8,128)(2,1)} custom-call(bf16[64,9,16,256]{3,2,1,0:T(8,128)(2,1)} %bitcast.1, bf16[64,128,128]{2,1,0:T(8,128)(2,1)} %tiles.1, s32[64]{0:T(128)} %dest_any.1, s32[64]{0:T(128)} %lev_any.1), custom_call_target="tpu_custom_call" | custom-call | tf_op jit(solution)/shard_map/pallas_call | solution.py:313
  77.7 3.5 %convert_element_type.3 = f32[64,3,16,256]{3,2,1,0:T(8,128)} convert(bf16[64,3,16,256]{3,2,1,0:T(8,128)(2,1)} %shard_map.46) | non-fusion elementwise | flops 786432 | bytes 4718592 | tf_op jit(solution)/shard_map/convert_element_type | solution.py:351

commit v3 on v2

--- a/solution.py
+++ b/solution.py
@@ -15,9 +15,13 @@
 BLOCKS = 64
 DEVS = 128
 AZ = 8
-R1 = 80
+FACES = 24
+EARLY = 44
 STRIDE = 107
 UNROLL = 4
+CUTS = (4, 16)
+GROUPS = 3
+GROUP = (DEVS - EARLY) // GROUPS
 NONE = 127
 
 
@@ -34,11 +38,24 @@
     return z * 4 + x, y * 2 + c
 
 
+def source_of(ax, az, i):
+    o = lax.rem(i * STRIDE, DEVS)
+    dc = lax.rem(o, 2)
+    dy = lax.rem(lax.div(o, 2), 4)
+    dx = lax.rem(lax.div(o, 8), 4)
+    dz = lax.div(o, 32)
+    z = lax.rem(lax.div(ax, 4) - dz + 4, 4)
+    x = lax.rem(lax.rem(ax, 4) - dx + 4, 4)
+    y = lax.rem(lax.div(az, 2) - dy + 4, 4)
+    c = lax.rem(lax.rem(az, 2) - dc + 2, 2)
+    return z * 4 + x, y * 2 + c
+
+
 def bf16_of(mask):
     return jnp.where(mask, 1.0, 0.0).astype(BF)
 
 
-def fill_constants(nsel, fsel, tsel, weights, ax):
+def fill_constants(nsel, fsel, spread, tsel, weights, ax):
     src = lax.broadcasted_iota(jnp.int32, (256, 256), 0)
     dst = lax.broadcasted_iota(jnp.int32, (256, 256), 1)
     ps, qs = lax.div(src, 16), lax.rem(src, 16)
@@ -65,7 +82,16 @@
         jnp.where(row < 32, 96 + row, lax.rem(row, 8) * 16 + jnp.where(row < 40, 0, 15)),
     )
     tsel[...] = bf16_of(col == pick)
-    kk = lax.rem(lax.broadcasted_iota(jnp.int32, (16, 128), 1), 64)
+    kk = lax.broadcasted_iota(jnp.int32, (64, 256), 0)
+    dst = lax.broadcasted_iota(jnp.int32, (64, 256), 1)
+    plane = jnp.where(kk < 48, 0, 8) + lax.rem(kk, 8)
+    pick = jnp.where(
+        kk < 16,
+        kk,
+        jnp.where(kk < 32, 224 + kk, plane * 16 + jnp.where(lax.rem(kk, 16) < 8, 0, 15)),
+    )
+    spread[...] = bf16_of(dst == pick)
+    kk = lax.rem(lax.broadcasted_iota(jnp.int32, (FACES, 128), 1), 64)
     weights[0] = bf16_of((kk < 16) & (ax > 0))
     weights[1] = bf16_of((kk >= 16) & (kk < 32) & (ax < 15))
     weights[2] = bf16_of((kk >= 32) & (lax.rem(kk, 16) < 8))
@@ -74,9 +100,10 @@
 
 def kernel(
     hist, tiles, dest_any, lev_any, out,
-    newest, older, tbuf, send1, recv1, base, send_a, recv_a, send_b, recv_b, stage, final, ordf,
-    nsel, fsel, tsel, weights, dest, lev, vidx, sidx, vinv, sinv,
-    load_sem, ssem, rsem, out_sem,
+    newest, older, tbuf, meta_s, meta_r, send1, recv1, send_t, recv_t, send2, recv2, base,
+    send_a, recv_a, send_b, recv_b, stage, final, ordf, beside_faces,
+    nsel, fsel, spread, tsel, weights, dest, lev, vidx, sidx, vinv, sinv,
+    load_sem, ssem, rsem, back_sem, out_sem,
 ):
     ax = lax.axis_index("ax")
     az = lax.axis_index("az")
@@ -117,10 +144,9 @@
     vidx[1:2, :] = slot
     to_smem = pltpu.make_async_copy(vidx, sidx, load_sem.at[2])
     to_smem.start()
-    fill_constants(nsel, fsel, tsel, weights, ax)
+    fill_constants(nsel, fsel, spread, tsel, weights, ax)
     to_smem.wait()
 
-    lanes16 = lax.broadcasted_iota(jnp.int32, (16, 128), 1)
 
     def scale_of(b):
         level = lev[b]
@@ -140,8 +166,7 @@
         defect = (source - (1.0 + 6.0 * c) * h0 + c * beside).astype(BF)
         lhs = jnp.concatenate([defect[:, 0:128], defect[:, 128:256]], axis=0)
         u = lax.dot_general(lhs, tbuf[b], (((1,), (1,)), ((), ())), preferred_element_type=F32)
-        moved = h0 + jnp.concatenate([u[0:48], u[48:96]], axis=1)
-        base[b] = moved.astype(BF).reshape(3, 16, 256)
+        return h0 + jnp.concatenate([u[0:48], u[48:96]], axis=1)
 
     def for_each(count, step):
         def some(n, carry):
@@ -151,23 +176,32 @@
 
         lax.fori_loop(0, count // UNROLL, some, 0)
 
-    row16 = lax.broadcasted_iota(jnp.int32, (16, 128), 0)
+    left16 = lax.broadcasted_iota(jnp.int32, (16, 128), 1) < 64
+    left8 = lax.broadcasted_iota(jnp.int32, (8, 128), 1) < 64
 
     def pack_first(d):
         below = jnp.maximum(d - AZ, 0)
         above = jnp.minimum(d + AZ, DEVS - 1)
         slot_below = jnp.where(d >= AZ, sidx[1, below], NONE)
         slot_above = jnp.where(d < DEVS - AZ, sidx[1, above], NONE)
-        slots = jnp.where(row16 == 0, sidx[1, d], jnp.where(row16 == 1, slot_below, slot_above))
+        meta_s[d] = jnp.where(lane < 64, sidx[1, d], slot_below * 128 + slot_above)
         own, low, high = sidx[0, d], sidx[0, below], sidx[0, above]
-        u = lax.dot_general(tsel[...], tbuf[own], (((1,), (1,)), ((), ())), preferred_element_type=F32)
-        send1[d, 0:48] = (u * scale_of(own)).astype(BF)
         faces = sum(
             jnp.dot(newest[b].reshape(48, 256), fsel[n], preferred_element_type=F32)
             for n, b in enumerate((low, high, own))
         )
-        send1[d, 48:64] = jnp.where(lanes16 < 64, faces[0:16], faces[16:32]).astype(BF)
-        send1[d, 64:80] = jnp.where(lanes16 < 64, faces[32:48], slots.astype(F32)).astype(BF)
+        upper = jnp.where(left16, faces[0:16], faces[16:32])
+        lower = jnp.where(left8, faces[32:40], faces[40:48])
+        send1[d] = jnp.concatenate([upper, lower], axis=0).astype(BF)
+
+    def columns_of(b):
+        u = lax.dot_general(tsel[...], tbuf[b], (((1,), (1,)), ((), ())), preferred_element_type=F32)
+        return (u * scale_of(b)).astype(BF)
+
+    def unfold(packed):
+        f = packed.astype(F32)
+        parts = [f[0:16, 0:64], f[0:16, 64:128], f[16:24, 0:64], f[16:24, 64:128]]
+        return jnp.concatenate(parts, axis=0).astype(BF)
 
     def push(src, dst, n, where):
         pltpu.make_async_remote_copy(
@@ -176,7 +210,6 @@
         ).start()
 
     load_h0.wait()
-    load_t.wait()
     pl.semaphore_wait(barrier, DEVS - 1)
 
     def send_first(n, carry):
@@ -184,88 +217,183 @@
         for tax, taz in targets:
             pack_first(tax * AZ + taz)
         for k, (tax, taz) in enumerate(targets):
+            d = tax * AZ + taz
+
+            def go():
+                push(meta_s.at[d], meta_r.at[me], 0, (tax, taz))
+                push(send1.at[d], recv1.at[me], 1, (tax, taz))
+
             if k > 0:
-                push(send1.at[tax * AZ + taz], recv1.at[me], 1, (tax, taz))
+                go()
             else:
-
-                @pl.when(n > 0)
-                def _():
-                    push(send1.at[tax * AZ + taz], recv1.at[me], 1, (tax, taz))
-
+                pl.when(n > 0)(go)
         return carry
 
     lax.fori_loop(0, DEVS // UNROLL, send_first, 0)
+    meta_r[me] = meta_s[me]
     recv1[me] = send1[me]
 
+    load_t.wait()
+
+    def each_target(low, high, make, go):
+        def some(n, carry):
+            items = [(n * UNROLL + k, target_of(ax, az, n * UNROLL + k)) for k in range(UNROLL)]
+            for i, (tax, taz) in items:
+                make(i, tax * AZ + taz)
+            for i, (tax, taz) in items:
+                go(i, tax * AZ + taz, (tax, taz))
+            return carry
+
+        lax.fori_loop(low // UNROLL, high // UNROLL, some, 0)
+
+    def make_columns(i, d):
+        send_t[i] = columns_of(sidx[0, d])
+
+    def go_columns(i, d, where):
+        pl.when(i > 0)(lambda: push(send_t.at[i], recv_t.at[me], 4, where))
+
+    each_target(0, EARLY, make_columns, go_columns)
+    recv_t[me] = send_t[0]
+
+    def no_columns(i, carry):
+        sax, saz = source_of(ax, az, i)
+        recv_t[sax * AZ + saz] = jnp.zeros((48, 128), BF)
+        return carry
+
+    lax.fori_loop(EARLY, DEVS, no_columns, 0)
+
     load_h.wait()
-    for_each(BLOCKS, base_part)
-    own = sidx[0, me]
-    recv_a[me] = base[own, 0:2]
-    recv_b[me] = base[own, 2:3]
-
-    def send_base(n, send, recv, low, high):
-        def one(i, carry):
-            tax, taz = target_of(ax, az, i)
-            d = tax * AZ + taz
-            send[d] = base[sidx[0, d], low:high]
-            push(send.at[d], recv.at[me], n, (tax, taz))
-            return carry
-
-        lax.fori_loop(1, DEVS, one, 0)
-
-    send_base(2, send_a, recv_a, 0, 2)
-
-    def all_of(ref, sem):
-        part = ref.at[pl.ds(0, DEVS - 1)]
+
+    def put(d, field):
+        field = field.astype(BF).reshape(3, 16, 256)
+        send_a[d] = field[0:2]
+        send_b[d] = field[2:3]
+
+    def make_base(i, d):
+        put(d, base_part(sidx[0, d]))
+
+    def go_base(i, d, where):
+        def go():
+            push(send_a.at[d], recv_a.at[me], 2, where)
+            push(send_b.at[d], recv_b.at[me], 3, where)
+
+        pl.when(i > 0)(go)
+
+    each_target(0, CUTS[0], make_base, go_base)
+    recv_a[me] = send_a[me]
+    recv_b[me] = send_b[me]
+
+    def all_of(ref, sem, count=DEVS - 1):
+        part = ref.at[pl.ds(0, count)]
         pltpu.make_async_copy(part, part, sem).wait()
 
-    all_of(recv1, rsem.at[1])
-
-    slot_of_lane = (lanes16 - 64).astype(F32)
-
-    def unplace(n, found):
+    all_of(meta_r, rsem.at[0])
+
+    def unplace(s, carry):
+        mine, low, high, slot_low, slot_high = carry
+        code = meta_r[s]
+        mine = jnp.where(code == lane, s, mine)
+        low = jnp.where(lax.div(code, 128) == lane - 64, s, low)
+        high = jnp.where(lax.rem(code, 128) == lane - 64, s, high)
+        slot_low = jnp.where(lane == s, code, slot_low)
+        slot_high = jnp.where(lane == s - 64, code, slot_high)
+        return mine, low, high, slot_low, slot_high
+
+    def unplace_some(n, carry):
         for k in range(UNROLL):
-            s = n * UNROLL + k
-            found = jnp.where(recv1[s, 64:80].astype(F32) == slot_of_lane, s, found)
-        return found
-
-    vinv[...] = lax.fori_loop(0, DEVS // UNROLL, unplace, jnp.zeros((16, 128), jnp.int32))
+            carry = unplace(n * UNROLL + k, carry)
+        return carry
+
+    nothing = (jnp.zeros((1, 128), jnp.int32),) * 5
+    found = lax.fori_loop(0, DEVS // UNROLL, unplace_some, nothing)
+    for n, row in enumerate(found):
+        vinv[n : n + 1, :] = row
     to_smem = pltpu.make_async_copy(vinv, sinv, load_sem.at[2])
     to_smem.start()
     to_smem.wait()
 
+    all_of(recv1, rsem.at[1])
+
     def order(j):
-        ordf[j + 1] = recv1[sinv[0, j + 64], 48:80]
+        ordf[j + 1] = recv1[sinv[0, j]]
 
     for_each(BLOCKS, order)
     edge_up = pltpu.make_async_remote_copy(
-        src_ref=ordf.at[BLOCKS], dst_ref=ordf.at[0], send_sem=ssem.at[4], recv_sem=rsem.at[4],
+        src_ref=ordf.at[BLOCKS], dst_ref=ordf.at[0], send_sem=ssem.at[6], recv_sem=rsem.at[6],
         device_id=(ax, lax.rem(az + 1, AZ)), device_id_type=MESH,
     )
     edge_down = pltpu.make_async_remote_copy(
-        src_ref=ordf.at[1], dst_ref=ordf.at[BLOCKS + 1], send_sem=ssem.at[5], recv_sem=rsem.at[5],
+        src_ref=ordf.at[1], dst_ref=ordf.at[BLOCKS + 1], send_sem=ssem.at[7], recv_sem=rsem.at[7],
         device_id=(ax, lax.rem(az + AZ - 1, AZ)), device_id_type=MESH,
     )
     edge_up.start()
     edge_down.start()
 
-    send_base(3, send_b, recv_b, 2, 3)
+    each_target(CUTS[0], CUTS[1], make_base, go_base)
     edge_up.wait_recv()
     edge_down.wait_recv()
 
+    def gather(j):
+        beside_faces[j] = (
+            recv1[sinv[1, j + 64]] * weights[0]
+            + recv1[sinv[2, j + 64]] * weights[1]
+            + ordf[j] * weights[2]
+            + ordf[j + 2] * weights[3]
+        )
+
+    for_each(BLOCKS, gather)
+
+    def send_back(group):
+        def one(i, carry):
+            sax, saz = source_of(ax, az, i)
+            s = sax * AZ + saz
+            slot = jnp.where(s < 64, sinv[3, jnp.minimum(s, 63)], sinv[4, jnp.maximum(s - 64, 0)])
+            send2[s] = beside_faces[jnp.minimum(slot, BLOCKS - 1)]
+            pltpu.make_async_remote_copy(
+                src_ref=send2.at[s], dst_ref=recv2.at[me], send_sem=ssem.at[5],
+                recv_sem=back_sem.at[group], device_id=(sax, saz), device_id_type=MESH,
+            ).start()
+            return carry
+
+        lax.fori_loop(EARLY + group * GROUP, EARLY + (group + 1) * GROUP, one, 0)
+
+    for group in range(GROUPS):
+        send_back(group)
+    each_target(CUTS[1], EARLY, make_base, go_base)
+
+    def keep_base(b):
+        base[b] = base_part(b)
+
+    for_each(BLOCKS, keep_base)
+
+    def finish(i, d):
+        b = sidx[0, d]
+        nearby = jnp.dot(unfold(recv2[d]), spread[...], preferred_element_type=F32).astype(BF)
+        lhs = jnp.concatenate([nearby[:, 0:128], nearby[:, 128:256]], axis=0)
+        u = lax.dot_general(lhs, tbuf[b], (((1,), (1,)), ((), ())), preferred_element_type=F32)
+        update = jnp.concatenate([u[0:48], u[48:96]], axis=1)
+        put(d, base[b] + (diffusion * scale_of(b)) * update)
+
+    def go_finished(i, d, where):
+        push(send_a.at[d], recv_a.at[me], 2, where)
+
+    for group in range(GROUPS):
+        all_of(recv2, back_sem.at[group], GROUP)
+        each_target(EARLY + group * GROUP, EARLY + (group + 1) * GROUP, finish, go_finished)
+
+    def send_rest(i, carry):
+        tax, taz = target_of(ax, az, i)
+        push(send_b.at[tax * AZ + taz], recv_b.at[me], 3, (tax, taz))
+        return carry
+
+    lax.fori_loop(EARLY, DEVS, send_rest, 0)
+
+    all_of(recv_t, rsem.at[4], EARLY - 1)
+
     def correct(j):
-        s, s_low, s_high = sinv[0, j + 64], sinv[1, j + 64], sinv[2, j + 64]
-        parts = []
-        for r in (0, 16):
-            parts.append(
-                recv1[s_low, 48 + r : 64 + r] * weights[0]
-                + recv1[s_high, 48 + r : 64 + r] * weights[1]
-                + ordf[j, r : r + 16] * weights[2]
-                + ordf[j + 2, r : r + 16] * weights[3]
-            )
-        lhs = jnp.concatenate([parts[0][:, 0:64], parts[0][:, 64:128], parts[1][:, 0:64]], axis=0)
+        s = sinv[0, j]
         none = jnp.zeros((16, 128), BF)
-        t_low, t_high, t_side = recv1[s, 0:16], recv1[s, 16:32], recv1[s, 32:48]
+        t_low, t_high, t_side = recv_t[s, 0:16], recv_t[s, 16:32], recv_t[s, 32:48]
         rhs = jnp.concatenate(
             [
                 jnp.concatenate([t_low, none, t_side, none], axis=0),
@@ -273,7 +401,7 @@
             ],
             axis=1,
         )
-        update = jnp.dot(lhs, rhs, preferred_element_type=F32) * diffusion
+        update = jnp.dot(unfold(beside_faces[j]), rhs, preferred_element_type=F32) * diffusion
         stage[j] = update.reshape(3, 16, 256)
 
     for_each(BLOCKS, correct)
@@ -281,7 +409,7 @@
     all_of(recv_a, rsem.at[2])
 
     def add_a(j):
-        final[j, 0:2] = (stage[j, 0:2] + recv_a[sinv[0, j + 64]].astype(F32)).astype(BF)
+        final[j, 0:2] = (stage[j, 0:2] + recv_a[sinv[0, j]].astype(F32)).astype(BF)
 
     for_each(BLOCKS, add_a)
     all_of(recv_b, rsem.at[3])
@@ -289,7 +417,7 @@
     def add_b(n, carry):
         for k in range(UNROLL):
             j = n * UNROLL + k
-            final[j, 2:3] = (stage[j, 2:3] + recv_b[sinv[0, j + 64]].astype(F32)).astype(BF)
+            final[j, 2:3] = (stage[j, 2:3] + recv_b[sinv[0, j]].astype(F32)).astype(BF)
         return carry
 
     copies = []
@@ -299,7 +427,10 @@
         copies.append(pltpu.make_async_copy(final.at[part], out.at[part], out_sem.at[g]))
         copies[-1].start()
 
+    all_of(meta_s, ssem.at[0])
     all_of(send1, ssem.at[1])
+    all_of(recv_t, ssem.at[4], EARLY - 1)
+    all_of(send2, ssem.at[5], DEVS - EARLY)
     all_of(send_a, ssem.at[2])
     all_of(send_b, ssem.at[3])
     edge_up.wait_send()
@@ -319,29 +450,38 @@
             pltpu.VMEM((BLOCKS, 3, 16, 256), BF),
             pltpu.VMEM((BLOCKS, 6, 16, 256), BF),
             pltpu.VMEM((BLOCKS, 128, 128), BF),
-            pltpu.VMEM((DEVS, R1, 128), BF),
-            pltpu.VMEM((DEVS, R1, 128), BF),
-            pltpu.VMEM((BLOCKS, 3, 16, 256), BF),
+            pltpu.VMEM((DEVS, 1, 128), jnp.int32),
+            pltpu.VMEM((DEVS, 1, 128), jnp.int32),
+            pltpu.VMEM((DEVS, FACES, 128), BF),
+            pltpu.VMEM((DEVS, FACES, 128), BF),
+            pltpu.VMEM((EARLY, 48, 128), BF),
+            pltpu.VMEM((DEVS, 48, 128), BF),
+            pltpu.VMEM((DEVS, FACES, 128), BF),
+            pltpu.VMEM((DEVS, FACES, 128), BF),
+            pltpu.VMEM((BLOCKS, 48, 256), F32),
             pltpu.VMEM((DEVS, 2, 16, 256), BF),
             pltpu.VMEM((DEVS, 2, 16, 256), BF),
             pltpu.VMEM((DEVS, 1, 16, 256), BF),
             pltpu.VMEM((DEVS, 1, 16, 256), BF),
             pltpu.VMEM((BLOCKS, 3, 16, 256), F32),
             pltpu.VMEM((BLOCKS, 3, 16, 256), BF),
-            pltpu.VMEM((BLOCKS + 2, 32, 128), BF),
+            pltpu.VMEM((BLOCKS + 2, FACES, 128), BF),
+            pltpu.VMEM((BLOCKS, FACES, 128), BF),
             pltpu.VMEM((256, 256), BF),
             pltpu.VMEM((3, 256, 128), BF),
+            pltpu.VMEM((64, 256), BF),
             pltpu.VMEM((48, 128), BF),
-            pltpu.VMEM((4, 16, 128), BF),
+            pltpu.VMEM((4, FACES, 128), BF),
             pltpu.SMEM((BLOCKS,), jnp.int32),
             pltpu.SMEM((BLOCKS,), jnp.int32),
             pltpu.VMEM((8, 128), jnp.int32),
             pltpu.SMEM((8, 128), jnp.int32),
-            pltpu.VMEM((16, 128), jnp.int32),
-            pltpu.SMEM((16, 128), jnp.int32),
+            pltpu.VMEM((8, 128), jnp.int32),
+            pltpu.SMEM((8, 128), jnp.int32),
             pltpu.SemaphoreType.DMA((6,)),
-            pltpu.SemaphoreType.DMA((6,)),
-            pltpu.SemaphoreType.DMA((6,)),
+            pltpu.SemaphoreType.DMA((8,)),
+            pltpu.SemaphoreType.DMA((8,)),
+            pltpu.SemaphoreType.DMA((GROUPS,)),
             pltpu.SemaphoreType.DMA((4,)),
         ],
         compiler_params=pltpu.CompilerParams(

time: 81.3 us -> 77.6 us (0.954)
  Pallas kernels: 77.7 us -> 73.9 us
    pallas_call x1, Pallas kernels: 77.7 us -> 73.9 us  [body(): pl.pallas_call(kernel, out_shape=jax.ShapeDtypeStruct((BLOCKS, 3, 16, 256...]
where the time goes in v3:
time: 77.6 us; the launch traced here: 77.5 us
  Pallas kernels  73.9 us (95%)
  other arithmetic  3.52 us (5%)
    pallas_call x1, Pallas kernels, body(): pl.pallas_call(kernel, out_shape=jax.ShapeDtypeStruct((BLOCKS, 3, 16, 256...  73.9 us
    convert_element_type x1, other arithmetic, body(): return moved.astype(F32)  3.52 us

profile of v3, /device:TPU:1, one launch (start us, length us, event | category | flops | bytes accessed | tf_op | source)
XLA Modules:
  0.0 77.5 jit_solution(1472910173472613777)
XLA Ops:
  0.0 73.9 %shard_map.46 = bf16[64,3,16,256]{3,2,1,0:T(8,128)(2,1)} custom-call(bf16[64,9,16,256]{3,2,1,0:T(8,128)(2,1)} %bitcast.1, bf16[64,128,128]{2,1,0:T(8,128)(2,1)} %tiles.1, s32[64]{0:T(128)} %dest_any.1, s32[64]{0:T(128)} %lev_any.1), custom_call_target="tpu_custom_call" | custom-call | tf_op jit(solution)/shard_map/pallas_call | solution.py:444
  73.9 3.5 %convert_element_type.3 = f32[64,3,16,256]{3,2,1,0:T(8,128)} convert(bf16[64,3,16,256]{3,2,1,0:T(8,128)(2,1)} %shard_map.46) | non-fusion elementwise | flops 786432 | bytes 4718592 | tf_op jit(solution)/shard_map/convert_element_type | solution.py:491

commit v4 on v3

--- a/solution.py
+++ b/solution.py
@@ -22,6 +22,7 @@
 CUTS = (4, 16)
 GROUPS = 3
 GROUP = (DEVS - EARLY) // GROUPS
+PARTS = 4
 NONE = 127
 
 
@@ -100,7 +101,7 @@
 
 def kernel(
     hist, tiles, dest_any, lev_any, out,
-    newest, older, tbuf, meta_s, meta_r, send1, recv1, send_t, recv_t, send2, recv2, base,
+    newest, older, tbuf, meta_s, meta_r, send1, recv1, send_t, recv_t, send2, recv2,
     send_a, recv_a, send_b, recv_b, stage, final, ordf, beside_faces,
     nsel, fsel, spread, tsel, weights, dest, lev, vidx, sidx, vinv, sinv,
     load_sem, ssem, rsem, back_sem, out_sem,
@@ -152,7 +153,7 @@
         level = lev[b]
         return jnp.where(level == 0, 1.0, jnp.where(level == 1, 4.0, 16.0)).astype(F32)
 
-    def base_part(b):
+    def swept(b, nearby=None):
         x = newest[b].reshape(48, 256)
         h0 = x.astype(F32)
         h1 = older[b, 0:3].reshape(48, 256).astype(F32)
@@ -163,6 +164,8 @@
         beside = jnp.dot(x, nsel[...], preferred_element_type=F32)
         beside += jnp.where(radial == 0, 0.0, pltpu.roll(h0, 1, 0))
         beside += jnp.where(radial == 15, 0.0, pltpu.roll(h0, 47, 0))
+        if nearby is not None:
+            beside += nearby
         defect = (source - (1.0 + 6.0 * c) * h0 + c * beside).astype(BF)
         lhs = jnp.concatenate([defect[:, 0:128], defect[:, 128:256]], axis=0)
         u = lax.dot_general(lhs, tbuf[b], (((1,), (1,)), ((), ())), preferred_element_type=F32)
@@ -270,7 +273,7 @@
         send_b[d] = field[2:3]
 
     def make_base(i, d):
-        put(d, base_part(sidx[0, d]))
+        put(d, swept(sidx[0, d]))
 
     def go_base(i, d, where):
         def go():
@@ -361,32 +364,27 @@
         send_back(group)
     each_target(CUTS[1], EARLY, make_base, go_base)
 
-    def keep_base(b):
-        base[b] = base_part(b)
-
-    for_each(BLOCKS, keep_base)
-
     def finish(i, d):
-        b = sidx[0, d]
-        nearby = jnp.dot(unfold(recv2[d]), spread[...], preferred_element_type=F32).astype(BF)
-        lhs = jnp.concatenate([nearby[:, 0:128], nearby[:, 128:256]], axis=0)
-        u = lax.dot_general(lhs, tbuf[b], (((1,), (1,)), ((), ())), preferred_element_type=F32)
-        update = jnp.concatenate([u[0:48], u[48:96]], axis=1)
-        put(d, base[b] + (diffusion * scale_of(b)) * update)
-
-    def go_finished(i, d, where):
+        nearby = jnp.dot(unfold(recv2[d]), spread[...], preferred_element_type=F32)
+        put(d, swept(sidx[0, d], nearby))
+
+    def go_whole(i, d, where):
+        push(send_a.at[d], recv_a.at[me], 2, where)
+        push(send_b.at[d], recv_b.at[me], 3, where)
+
+    def go_first(i, d, where):
         push(send_a.at[d], recv_a.at[me], 2, where)
 
     for group in range(GROUPS):
         all_of(recv2, back_sem.at[group], GROUP)
-        each_target(EARLY + group * GROUP, EARLY + (group + 1) * GROUP, finish, go_finished)
+        each_target(EARLY + group * GROUP, EARLY + (group + 1) * GROUP, finish, go_whole if group < GROUPS - 1 else go_first)
 
     def send_rest(i, carry):
         tax, taz = target_of(ax, az, i)
         push(send_b.at[tax * AZ + taz], recv_b.at[me], 3, (tax, taz))
         return carry
 
-    lax.fori_loop(EARLY, DEVS, send_rest, 0)
+    lax.fori_loop(DEVS - GROUP, DEVS, send_rest, 0)
 
     all_of(recv_t, rsem.at[4], EARLY - 1)
 
@@ -437,6 +435,28 @@
     edge_down.wait_send()
     for copy in copies:
         copy.wait()
+
+
+def widen(narrow, wide, held, widened, in_sem, out_sem):
+    size = BLOCKS // PARTS
+    parts = [pl.ds(n * size, size) for n in range(PARTS)]
+    loads = [pltpu.make_async_copy(narrow.at[p], held.at[p], in_sem.at[n]) for n, p in enumerate(parts)]
+    stores = [pltpu.make_async_copy(widened.at[p], wide.at[p], out_sem.at[n]) for n, p in enumerate(parts)]
+    for load in loads:
+        load.start()
+    for n in range(PARTS):
+        loads[n].wait()
+
+        def one(j, carry):
+            for k in range(UNROLL):
+                b = n * size + j * UNROLL + k
+                widened[b] = held[b].astype(F32)
+            return carry
+
+        lax.fori_loop(0, size // UNROLL, one, 0)
+        stores[n].start()
+    for store in stores:
+        store.wait()
 
 
 def body(history, inverse_tiles, levels, destination):
@@ -458,7 +478,6 @@
             pltpu.VMEM((DEVS, 48, 128), BF),
             pltpu.VMEM((DEVS, FACES, 128), BF),
             pltpu.VMEM((DEVS, FACES, 128), BF),
-            pltpu.VMEM((BLOCKS, 48, 256), F32),
             pltpu.VMEM((DEVS, 2, 16, 256), BF),
             pltpu.VMEM((DEVS, 2, 16, 256), BF),
             pltpu.VMEM((DEVS, 1, 16, 256), BF),
@@ -488,7 +507,19 @@
             collective_id=0, has_side_effects=True, vmem_limit_bytes=60 * 2**20
         ),
     )(history.reshape(BLOCKS, 9, 16, 256), inverse_tiles, destination, levels)
-    return moved.astype(F32)
+    return pl.pallas_call(
+        widen,
+        out_shape=jax.ShapeDtypeStruct((BLOCKS, 3, 16, 256), F32),
+        in_specs=[pl.BlockSpec(memory_space=pltpu.HBM)],
+        out_specs=pl.BlockSpec(memory_space=pltpu.HBM),
+        scratch_shapes=[
+            pltpu.VMEM((BLOCKS, 3, 16, 256), BF),
+            pltpu.VMEM((BLOCKS, 3, 16, 256), F32),
+            pltpu.SemaphoreType.DMA((PARTS,)),
+            pltpu.SemaphoreType.DMA((PARTS,)),
+        ],
+        compiler_params=pltpu.CompilerParams(vmem_limit_bytes=60 * 2**20),
+    )(moved)
 
 
 def solution(mesh):

time: 77.6 us -> 77 us (level)
  other arithmetic: 3.52 us -> 0 us
  Pallas kernels: 73.9 us -> 76.9 us
    convert_element_type x1 -> x0, other arithmetic: 3.52 us -> none  [body(): return moved.astype(F32)]
    pallas_call x0 -> x1, Pallas kernels: none -> 2.78 us  [body(): pl.pallas_call(widen, out_shape=jax.ShapeDtypeStruct((BLOCKS, 3, 16, 256)...]
where the time goes in v4:
time: 77 us; the launch traced here: 76.9 us
  Pallas kernels  76.9 us (100%)
    pallas_call x1, Pallas kernels, body(): pl.pallas_call(kernel, out_shape=jax.ShapeDtypeStruct((BLOCKS, 3, 16, 256...  74.1 us
    pallas_call x1, Pallas kernels, body(): pl.pallas_call(widen, out_shape=jax.ShapeDtypeStruct((BLOCKS, 3, 16, 256)...  2.78 us

profile of v4, /device:TPU:1, one launch (start us, length us, event | category | flops | bytes accessed | tf_op | source)
XLA Modules:
  0.0 76.9 jit_solution(4861219971141328062)
XLA Ops:
  0.0 74.1 %shard_map.46.narrow = bf16[64,3,16,256]{3,2,1,0:T(8,128)(2,1)} custom-call(bf16[64,9,16,256]{3,2,1,0:T(8,128)(2,1)} %bitcast.1, bf16[64,128,128]{2,1,0:T(8,128)(2,1)} %tiles.1, s32[64]{0:T(128)} %dest_any.1, s32[64]{0:T(128)} %lev_any.1), custom_call_target="tpu_custom_call" | custom-call | tf_op jit(solution)/shard_map/pallas_call | solution.py:464
  74.1 2.8 %shard_map.47 = f32[64,3,16,256]{3,2,1,0:T(8,128)} custom-call(bf16[64,3,16,256]{3,2,1,0:T(8,128)(2,1)} %shard_map.46.narrow), custom_call_target="tpu_custom_call" | custom-call | tf_op jit(solution)/shard_map/pallas_call | solution.py:510

commit v5 on v4

--- a/solution.py
+++ b/solution.py
@@ -17,9 +17,9 @@
 AZ = 8
 FACES = 24
 EARLY = 44
-STRIDE = 107
+STRIDE = 81
 UNROLL = 4
-CUTS = (4, 16)
+CUTS = (8, 24)
 GROUPS = 3
 GROUP = (DEVS - EARLY) // GROUPS
 PARTS = 4

time: 77 us -> 75.1 us (0.975)
  Pallas kernels: 76.9 us -> 74.8 us
    pallas_call x1, Pallas kernels: 74.1 us -> 72 us  [body(): pl.pallas_call(kernel, out_shape=jax.ShapeDtypeStruct((BLOCKS, 3, 16, 256...]
where the time goes in v5:
time: 75.1 us; the launch traced here: 74.8 us
  Pallas kernels  74.8 us (100%)
    pallas_call x1, Pallas kernels, body(): pl.pallas_call(kernel, out_shape=jax.ShapeDtypeStruct((BLOCKS, 3, 16, 256...  72 us
    pallas_call x1, Pallas kernels, body(): pl.pallas_call(widen, out_shape=jax.ShapeDtypeStruct((BLOCKS, 3, 16, 256)...  2.78 us

profile of v5, /device:TPU:1, one launch (start us, length us, event | category | flops | bytes accessed | tf_op | source)
XLA Modules:
  0.0 74.8 jit_solution(18421052562195962312)
XLA Ops:
  0.0 72.0 %shard_map.46.narrow = bf16[64,3,16,256]{3,2,1,0:T(8,128)(2,1)} custom-call(bf16[64,9,16,256]{3,2,1,0:T(8,128)(2,1)} %bitcast.1, bf16[64,128,128]{2,1,0:T(8,128)(2,1)} %tiles.1, s32[64]{0:T(128)} %dest_any.1, s32[64]{0:T(128)} %lev_any.1), custom_call_target="tpu_custom_call" | custom-call | tf_op jit(solution)/shard_map/pallas_call | solution.py:464
  72.0 2.8 %shard_map.47 = f32[64,3,16,256]{3,2,1,0:T(8,128)} custom-call(bf16[64,3,16,256]{3,2,1,0:T(8,128)(2,1)} %shard_map.46.narrow), custom_call_target="tpu_custom_call" | custom-call | tf_op jit(solution)/shard_map/pallas_call | solution.py:510

commit v6 on v5

--- a/solution.py
+++ b/solution.py
@@ -16,10 +16,10 @@
 DEVS = 128
 AZ = 8
 FACES = 24
-EARLY = 44
+EARLY = 32
 STRIDE = 81
 UNROLL = 4
-CUTS = (8, 24)
+CUTS = (8, 20)
 GROUPS = 3
 GROUP = (DEVS - EARLY) // GROUPS
 PARTS = 4

time: 75.1 us -> 75 us (level)
  no operation moved by 1% of the time
where the time goes in v6:
time: 75 us; the launch traced here: 74.8 us
  Pallas kernels  74.8 us (100%)
    pallas_call x1, Pallas kernels, body(): pl.pallas_call(kernel, out_shape=jax.ShapeDtypeStruct((BLOCKS, 3, 16, 256...  72 us
    pallas_call x1, Pallas kernels, body(): pl.pallas_call(widen, out_shape=jax.ShapeDtypeStruct((BLOCKS, 3, 16, 256)...  2.78 us

profile of v6, /device:TPU:1, one launch (start us, length us, event | category | flops | bytes accessed | tf_op | source)
XLA Modules:
  0.0 74.8 jit_solution(8406817398388653356)
XLA Ops:
  0.0 72.0 %shard_map.46.narrow = bf16[64,3,16,256]{3,2,1,0:T(8,128)(2,1)} custom-call(bf16[64,9,16,256]{3,2,1,0:T(8,128)(2,1)} %bitcast.1, bf16[64,128,128]{2,1,0:T(8,128)(2,1)} %tiles.1, s32[64]{0:T(128)} %dest_any.1, s32[64]{0:T(128)} %lev_any.1), custom_call_target="tpu_custom_call" | custom-call | tf_op jit(solution)/shard_map/pallas_call | solution.py:464
  72.1 2.8 %shard_map.47 = f32[64,3,16,256]{3,2,1,0:T(8,128)} custom-call(bf16[64,3,16,256]{3,2,1,0:T(8,128)(2,1)} %shard_map.46.narrow), custom_call_target="tpu_custom_call" | custom-call | tf_op jit(solution)/shard_map/pallas_call | solution.py:510

commit v7 on v5

--- a/solution.py
+++ b/solution.py
@@ -121,7 +121,7 @@
         load.start()
 
     def greet(i, carry):
-        t = lax.rem(me + i, DEVS)
+        t = jnp.where(i - 1 < me, i - 1, i)
         there = (lax.div(t, AZ), lax.rem(t, AZ))
         pl.semaphore_signal(barrier, inc=1, device_id=there, device_id_type=MESH)
         return carry

time: 75.1 us -> 75.3 us (level)
  no operation moved by 1% of the time
where the time goes in v7:
time: 75.3 us; the launch traced here: 75.2 us
  Pallas kernels  75.1 us (100%)
    pallas_call x1, Pallas kernels, body(): pl.pallas_call(kernel, out_shape=jax.ShapeDtypeStruct((BLOCKS, 3, 16, 256...  72.4 us
    pallas_call x1, Pallas kernels, body(): pl.pallas_call(widen, out_shape=jax.ShapeDtypeStruct((BLOCKS, 3, 16, 256)...  2.78 us

profile of v7, /device:TPU:1, one launch (start us, length us, event | category | flops | bytes accessed | tf_op | source)
XLA Modules:
  0.0 75.2 jit_solution(4737684181174167263)
XLA Ops:
  0.0 72.4 %shard_map.46.narrow = bf16[64,3,16,256]{3,2,1,0:T(8,128)(2,1)} custom-call(bf16[64,9,16,256]{3,2,1,0:T(8,128)(2,1)} %bitcast.1, bf16[64,128,128]{2,1,0:T(8,128)(2,1)} %tiles.1, s32[64]{0:T(128)} %dest_any.1, s32[64]{0:T(128)} %lev_any.1), custom_call_target="tpu_custom_call" | custom-call | tf_op jit(solution)/shard_map/pallas_call | solution.py:464
  72.4 2.8 %shard_map.47 = f32[64,3,16,256]{3,2,1,0:T(8,128)} custom-call(bf16[64,3,16,256]{3,2,1,0:T(8,128)(2,1)} %shard_map.46.narrow), custom_call_target="tpu_custom_call" | custom-call | tf_op jit(solution)/shard_map/pallas_call | solution.py:510
